TPU v7x, 256 devices: a whole 4x4x8 slice. The times are simulated.
256 devices in a mesh: section: 4 (over x), ctx: 32 (over z, y), tp: 2 (over core).
Axes of the slice: x: 4, y: 4, z: 8, core: 2. Of those that a mesh axis runs over, the one named last changes fastest.
Arguments:
- queries: bfloat16 [4, 8192, 64, 128], P('section', 'ctx', 'tp'), may hold values from -6 to 6
- key_heads: bfloat16 [4, 8192, 8, 128], P('section', 'ctx', 'tp'), may hold values from -6 to 6
- section_values: bfloat16 [4, 8192, 8, 128], P('section', 'ctx', 'tp'), may hold values from -6 to 6
- block_docs: int32 [64], replicated, may hold values from 0 to 15, never falling along the last dimension, each value on 1 to 15 neighbouring positions
Outputs:
- handed: bfloat16 [4, 8192, 8192], P('section', 'ctx', 'tp')
Inputs may be any that keep to these rules, and one draw needn't show every extreme that they name: `block_docs`: numbers never fall along the sequence; every document covers 1 to 15 consecutive blocks and one covers exactly 15.
All inputs are finite; a program needn't handle non-finite values.
Results may differ from a plain program's by a relative error of at most 0.004.
Values may be sent and summed in bfloat16 or wider, within the bound.
A program may use at most 128 MiB of HBM per device.

v0:
```python
import math

import jax
import jax.numpy as jnp
from jax import lax
from jax.sharding import PartitionSpec as P

BLK = 128


LOW_SCORE = -1e30


def passed_along(value, axis, steps):
    count = lax.axis_size(axis)
    leading, last = (max(0, -steps), min(count, count - steps))
    return lax.ppermute(value, axis, [(source, source + steps) for source in range(leading, last)])


def shifted(shard, axis, by):
    peers = lax.axis_size(axis)
    return lax.ppermute(shard, axis, [(i, (i + by) % peers) for i in range(peers)])


def absorb(
    running, paired, key_first, grouped_heads, query_docs, query_spots, padded_docs, pad_blocks
):
    key_count = paired.shape[1]
    stride = math.gcd(key_count, 512)
    scale = 1.0 / math.sqrt(grouped_heads.shape[-1])

    def visit(block_index, carry):
        offset = block_index * stride
        block_first = key_first + offset
        key_spots = block_first + jnp.arange(stride, dtype=jnp.int32)
        lead_block = block_first // BLK + pad_blocks
        key_docs = jnp.repeat(lax.dynamic_slice_in_dim(padded_docs, lead_block, stride // BLK), BLK)
        allowed = (
            (query_docs[:, None] == key_docs[None, :])
            & (key_spots[None, :] <= query_spots[:, None])
            & (key_spots[None, :] >= 0)
        )

        def update(current):
            row_peak, row_total, mixture = current
            scores = (
                jnp.einsum(
                    "tgjd,kgd->tgjk", grouped_heads, paired[0], preferred_element_type=jnp.float32
                )
                * scale
            )
            inside = allowed[:, None, None, :]
            masked = jnp.where(inside, scores, LOW_SCORE)
            new_peak = jnp.maximum(row_peak, jnp.max(masked, axis=-1))
            weight = jnp.where(inside, jnp.exp(masked - new_peak[..., None]), 0.0)
            factor = jnp.exp(row_peak - new_peak)
            row_total = row_total * factor + jnp.sum(weight, axis=-1)
            mixture = mixture * factor[..., None] + jnp.einsum(
                "tgjk,kgd->tgjd",
                weight.astype(jnp.bfloat16),
                paired[1],
                preferred_element_type=jnp.float32,
            )
            return (new_peak, row_total, mixture)

        def keep(current):
            return current

        return lax.cond(jnp.any(allowed), update, keep, carry)

    return lax.fori_loop(0, key_count // stride, visit, running)


def local(queries, key_heads, section_values, block_docs):
    ctx_count = lax.axis_size("ctx")
    cycle_index = lax.axis_index("ctx")
    reach_span = min(8, ctx_count)
    count_of_rows = queries.shape[1]
    head_count = queries.shape[2]
    kv_count = key_heads.shape[2]
    head_dim = queries.shape[3]
    group_width = head_count // kv_count
    grouped_heads = queries[0].reshape(count_of_rows, kv_count, group_width, head_dim)
    own_first = cycle_index * count_of_rows
    query_spots = own_first + jnp.arange(count_of_rows, dtype=jnp.int32)
    query_docs = jnp.repeat(
        lax.dynamic_slice_in_dim(block_docs, own_first // BLK, count_of_rows // BLK), BLK
    )
    pad_blocks = (reach_span - 1) * count_of_rows // BLK
    padded_docs = jnp.concatenate((jnp.full((pad_blocks,), -1, jnp.int32), block_docs))
    paired = jnp.stack((key_heads[0], section_values[0]))
    running = (
        jnp.full((count_of_rows, kv_count, group_width), LOW_SCORE, jnp.float32),
        jnp.zeros((count_of_rows, kv_count, group_width), jnp.float32),
        jnp.zeros((count_of_rows, kv_count, group_width, head_dim), jnp.float32),
    )

    def absorb_piece(carry, pieces, key_first):
        return absorb(
            carry,
            pieces,
            key_first,
            grouped_heads,
            query_docs,
            query_spots,
            padded_docs,
            pad_blocks,
        )

    running = absorb_piece(running, paired, own_first)

    def hop(step_index, carry):
        partial_value, moving = carry
        moving = passed_along(moving, "ctx", 1)
        partial_value = absorb_piece(
            partial_value, moving, own_first - (step_index + 1) * count_of_rows
        )
        return (partial_value, moving)

    running, unused = lax.fori_loop(0, reach_span - 1, hop, (running, paired))
    row_peak, row_total, mixture = running
    attention = (
        (mixture / row_total[..., None])
        .reshape(count_of_rows, head_count * head_dim)
        .astype(jnp.bfloat16)
    )
    return shifted(attention[None], "section", 1)


def solution(mesh):
    in_specs = (
        P("section", "ctx", "tp", None),
        P("section", "ctx", "tp", None),
        P("section", "ctx", "tp", None),
        P(),
    )
    out_specs = P("section", "ctx", "tp")
    return jax.shard_map(local, mesh=mesh, in_specs=in_specs, out_specs=out_specs, check_vma=False)
```

profile of v0, /device:TPU:56, one launch (start us, length us, event | category | flops | bytes accessed | tf_op | source)
XLA Modules:
  0.0 235.8 jit_solution(3217637646200371008)
XLA Ops:
  3.1 2.4 %copy.7 = bf16[1,256,32,128]{3,1,2,0:T(8,128)(2,1)S(1)} copy(bf16[1,256,32,128]{3,2,1,0:T(8,128)(2,1)} %param.10) | data formatting | bytes 4194304 | tf_op args[0]
  7.5 2.4 %broadcast_in_dim.85 = f32[256,4,8,128]{3,0,2,1:T(8,128)} broadcast(f32[]{:T(128)} %constant.188.clone.1), dimensions={} | broadcast | bytes 4194308 | tf_op jit(solution)/shard_map/broadcast_in_dim | solution.py:95
  10.0 9.8 %conditional.2 = ((f32[256,4,8]{0,2,1:T(8,128)S(1)}, f32[256,4,8]{0,2,1:T(8,128)S(1)}, f32[256,4,8,128]{3,0,2,1:T(8,128)})) conditional(s32[]{:T(128)} %convert_element_type.34, (f32[256,4,8]{0,2,1:T(8,128)S(1)}, f32[256,4,8]{0,2,1:T(8,128)S(1)}, f32[256,4,8,128]{3,0,2,1:T(8,128)}) %tuple.47, (pred[256,256]{0,1:T(8,128)(4,1)S(1)}, ...), branch_computations={%region_1.2_spmd, %region_2.5_spmd} | conditional | flops 1103118336 | bytes 70451288 | solution.py:69
  11.4 2.1 fusion.6
  13.6 4.2 %bitcast_add_fusion = f32[256,4,8,128]{3,0,2,1:T(8,128)S(1)} fusion(f32[256,4,8,128]{3,0,2,1:T(8,128)S(1)} %copy-done, f32[256,4,8]{0,2,1:T(8,128)S(1)} %get-tuple-element.498, f32[4,256,256,8]{2,1,3,0:T(8,128)S(1)} %get-tuple-element.506, f32[256,4,8]{0,2,1:T(8,128)S(1)} %max.4, pred[256,256]{0,1:T(8,128)(4,1)S(1)} %get-tuple-element.382, ...), kind=kOutput, calls=%fused_computation.8 | convolution fusion | flops 549453824 | bytes 17170432 | tf_op jit(solution)/shard_map/while/body/eval_jaxpr/cond/branch_1_fun/tgjk,kgd->tgjd/dot_general | solution.py:58
  17.8 1.9 copy-done.1
  19.7 163.5 %while.45 = (s32[]{:T(128)}, f32[256,4,8]{0,2,1:T(8,128)S(1)}, f32[256,4,8]{0,2,1:T(8,128)S(1)}, f32[256,4,8,128]{3,0,2,1:T(8,128)}, bf16[2,256,4,128]{3,1,2,0:T...) while((s32[]{:T(128)}, f32[256,4,8]{0,2,1:T(8,128)S(1)}, ...), condition=%wide.region_11.12_spmd.clone.clone, body=%wide.region_5.11_spmd.clone.clone.sunk | while | flops 1103447040 | bytes 73671800 | solution.py:120
  19.7 3.5 %collective-permute-start = (bf16[2,256,4,128]{3,1,2,0:T(8,128)(2,1)S(1)}, bf16[2,256,4,128]{3,1,2,0:T(8,128)(2,1)S(1)}, u32[]{:S(2)}, u32[]{:S(2)}) collective-permute-start(bf16[2,256,4,128]{3,1,2,0:T(8,128)(2,1)S(1)} %get-tuple-element.611), channel_id=1, source_target_pairs={{0,2},{2,4},{4,6},{6,8},{8,10},{10,12},{12,14},{14,16},{16,18},{18... | collective-permute-start | bytes 1572872 | tf_op jit(solution)/shard_map/while/body/eval_jaxpr/ppermute | solution.py:17
  24.9 10.3 %collective-permute-done = bf16[2,256,4,128]{3,1,2,0:T(8,128)(2,1)S(1)} collective-permute-done((bf16[2,256,4,128]{3,1,2,0:T(8,128)(2,1)S(1)}, bf16[2,256,4,128]{3,1,2,0:T(8,128)(2,1)S(1)}, u32[]{:S(2)}, u32[]{:S(2)}) %collective-permute-start) | collective-permute-done | bytes 524320 | tf_op jit(solution)/shard_map/while/body/eval_jaxpr/ppermute | solution.py:17
  35.3 9.6 %conditional.6 = ((f32[256,4,8]{0,2,1:T(8,128)S(1)}, f32[256,4,8]{0,2,1:T(8,128)S(1)}, f32[256,4,8,128]{3,0,2,1:T(8,128)})) conditional(s32[]{:T(128)} %convert_element_type.49, (f32[256,4,8]{0,2,1:T(8,128)S(1)}, f32[256,4,8]{0,2,1:T(8,128)S(1)}, f32[256,4,8,128]{3,0,2,1:T(8,128)}) %tuple.81, (pred[256,256]{0,1:T(8,128)(4,1)S(1)}, ...), branch_computations={%region_7.7_spmd, %region_8.10_spmd} | conditional | flops 1103118336 | bytes 70451288 | solution.py:69
  36.6 2.1 fusion.26
  38.8 4.1 %bitcast_add_fusion.1 = f32[256,4,8,128]{3,0,2,1:T(8,128)S(1)} fusion(f32[256,4,8,128]{3,0,2,1:T(8,128)S(1)} %copy-done.2, f32[256,4,8]{0,2,1:T(8,128)S(1)} %get-tuple-element.500, f32[4,256,256,8]{2,1,3,0:T(8,128)S(1)} %get-tuple-element.508, f32[256,4,8]{0,2,1:T(8,128)S(1)} %max.5, pred[256,256]{0,1:T(8,128)(4,1)S(1)} %get-tuple-element.389, ...), kind=kOutput, calls=%fused_computation.30 | convolution fusion | flops 549453824 | bytes 17170432 | tf_op jit(solution)/shard_map/while/body/eval_jaxpr/while/body/eval_jaxpr/cond/branch_1_fun/tgjk,kgd->tgjd/dot_general | solution.py:58
  43.0 1.9 copy-done.3
  48.6 11.0 %collective-permute-done = bf16[2,256,4,128]{3,1,2,0:T(8,128)(2,1)S(1)} collective-permute-done((bf16[2,256,4,128]{3,1,2,0:T(8,128)(2,1)S(1)}, bf16[2,256,4,128]{3,1,2,0:T(8,128)(2,1)S(1)}, u32[]{:S(2)}, u32[]{:S(2)}) %collective-permute-start) | collective-permute-done | bytes 524320 | tf_op jit(solution)/shard_map/while/body/eval_jaxpr/ppermute | solution.py:17
  59.6 9.6 %conditional.6 = ((f32[256,4,8]{0,2,1:T(8,128)S(1)}, f32[256,4,8]{0,2,1:T(8,128)S(1)}, f32[256,4,8,128]{3,0,2,1:T(8,128)})) conditional(s32[]{:T(128)} %convert_element_type.49, (f32[256,4,8]{0,2,1:T(8,128)S(1)}, f32[256,4,8]{0,2,1:T(8,128)S(1)}, f32[256,4,8,128]{3,0,2,1:T(8,128)}) %tuple.81, (pred[256,256]{0,1:T(8,128)(4,1)S(1)}, ...), branch_computations={%region_7.7_spmd, %region_8.10_spmd} | conditional | flops 1103118336 | bytes 70451288 | solution.py:69
  61.0 2.1 fusion.26
  63.2 4.1 %bitcast_add_fusion.1 = f32[256,4,8,128]{3,0,2,1:T(8,128)S(1)} fusion(f32[256,4,8,128]{3,0,2,1:T(8,128)S(1)} %copy-done.2, f32[256,4,8]{0,2,1:T(8,128)S(1)} %get-tuple-element.500, f32[4,256,256,8]{2,1,3,0:T(8,128)S(1)} %get-tuple-element.508, f32[256,4,8]{0,2,1:T(8,128)S(1)} %max.5, pred[256,256]{0,1:T(8,128)(4,1)S(1)} %get-tuple-element.389, ...), kind=kOutput, calls=%fused_computation.30 | convolution fusion | flops 549453824 | bytes 17170432 | tf_op jit(solution)/shard_map/while/body/eval_jaxpr/while/body/eval_jaxpr/cond/branch_1_fun/tgjk,kgd->tgjd/dot_general | solution.py:58
  67.3 1.9 copy-done.3
  73.0 10.1 %collective-permute-done = bf16[2,256,4,128]{3,1,2,0:T(8,128)(2,1)S(1)} collective-permute-done((bf16[2,256,4,128]{3,1,2,0:T(8,128)(2,1)S(1)}, bf16[2,256,4,128]{3,1,2,0:T(8,128)(2,1)S(1)}, u32[]{:S(2)}, u32[]{:S(2)}) %collective-permute-start) | collective-permute-done | bytes 524320 | tf_op jit(solution)/shard_map/while/body/eval_jaxpr/ppermute | solution.py:17
  83.1 9.6 %conditional.6 = ((f32[256,4,8]{0,2,1:T(8,128)S(1)}, f32[256,4,8]{0,2,1:T(8,128)S(1)}, f32[256,4,8,128]{3,0,2,1:T(8,128)})) conditional(s32[]{:T(128)} %convert_element_type.49, (f32[256,4,8]{0,2,1:T(8,128)S(1)}, f32[256,4,8]{0,2,1:T(8,128)S(1)}, f32[256,4,8,128]{3,0,2,1:T(8,128)}) %tuple.81, (pred[256,256]{0,1:T(8,128)(4,1)S(1)}, ...), branch_computations={%region_7.7_spmd, %region_8.10_spmd} | conditional | flops 1103118336 | bytes 70451288 | solution.py:69
  84.4 2.1 fusion.26
  86.6 4.1 %bitcast_add_fusion.1 = f32[256,4,8,128]{3,0,2,1:T(8,128)S(1)} fusion(f32[256,4,8,128]{3,0,2,1:T(8,128)S(1)} %copy-done.2, f32[256,4,8]{0,2,1:T(8,128)S(1)} %get-tuple-element.500, f32[4,256,256,8]{2,1,3,0:T(8,128)S(1)} %get-tuple-element.508, f32[256,4,8]{0,2,1:T(8,128)S(1)} %max.5, pred[256,256]{0,1:T(8,128)(4,1)S(1)} %get-tuple-element.389, ...), kind=kOutput, calls=%fused_computation.30 | convolution fusion | flops 549453824 | bytes 17170432 | tf_op jit(solution)/shard_map/while/body/eval_jaxpr/while/body/eval_jaxpr/cond/branch_1_fun/tgjk,kgd->tgjd/dot_general | solution.py:58
  90.8 1.9 copy-done.3
  96.4 9.2 %collective-permute-done = bf16[2,256,4,128]{3,1,2,0:T(8,128)(2,1)S(1)} collective-permute-done((bf16[2,256,4,128]{3,1,2,0:T(8,128)(2,1)S(1)}, bf16[2,256,4,128]{3,1,2,0:T(8,128)(2,1)S(1)}, u32[]{:S(2)}, u32[]{:S(2)}) %collective-permute-start) | collective-permute-done | bytes 524320 | tf_op jit(solution)/shard_map/while/body/eval_jaxpr/ppermute | solution.py:17
  105.6 9.6 %conditional.6 = ((f32[256,4,8]{0,2,1:T(8,128)S(1)}, f32[256,4,8]{0,2,1:T(8,128)S(1)}, f32[256,4,8,128]{3,0,2,1:T(8,128)})) conditional(s32[]{:T(128)} %convert_element_type.49, (f32[256,4,8]{0,2,1:T(8,128)S(1)}, f32[256,4,8]{0,2,1:T(8,128)S(1)}, f32[256,4,8,128]{3,0,2,1:T(8,128)}) %tuple.81, (pred[256,256]{0,1:T(8,128)(4,1)S(1)}, ...), branch_computations={%region_7.7_spmd, %region_8.10_spmd} | conditional | flops 1103118336 | bytes 70451288 | solution.py:69
  107.0 2.1 fusion.26
  109.1 4.1 %bitcast_add_fusion.1 = f32[256,4,8,128]{3,0,2,1:T(8,128)S(1)} fusion(f32[256,4,8,128]{3,0,2,1:T(8,128)S(1)} %copy-done.2, f32[256,4,8]{0,2,1:T(8,128)S(1)} %get-tuple-element.500, f32[4,256,256,8]{2,1,3,0:T(8,128)S(1)} %get-tuple-element.508, f32[256,4,8]{0,2,1:T(8,128)S(1)} %max.5, pred[256,256]{0,1:T(8,128)(4,1)S(1)} %get-tuple-element.389, ...), kind=kOutput, calls=%fused_computation.30 | convolution fusion | flops 549453824 | bytes 17170432 | tf_op jit(solution)/shard_map/while/body/eval_jaxpr/while/body/eval_jaxpr/cond/branch_1_fun/tgjk,kgd->tgjd/dot_general | solution.py:58
  113.3 1.9 copy-done.3
  118.9 9.8 %collective-permute-done = bf16[2,256,4,128]{3,1,2,0:T(8,128)(2,1)S(1)} collective-permute-done((bf16[2,256,4,128]{3,1,2,0:T(8,128)(2,1)S(1)}, bf16[2,256,4,128]{3,1,2,0:T(8,128)(2,1)S(1)}, u32[]{:S(2)}, u32[]{:S(2)}) %collective-permute-start) | collective-permute-done | bytes 524320 | tf_op jit(solution)/shard_map/while/body/eval_jaxpr/ppermute | solution.py:17
  128.7 9.6 %conditional.6 = ((f32[256,4,8]{0,2,1:T(8,128)S(1)}, f32[256,4,8]{0,2,1:T(8,128)S(1)}, f32[256,4,8,128]{3,0,2,1:T(8,128)})) conditional(s32[]{:T(128)} %convert_element_type.49, (f32[256,4,8]{0,2,1:T(8,128)S(1)}, f32[256,4,8]{0,2,1:T(8,128)S(1)}, f32[256,4,8,128]{3,0,2,1:T(8,128)}) %tuple.81, (pred[256,256]{0,1:T(8,128)(4,1)S(1)}, ...), branch_computations={%region_7.7_spmd, %region_8.10_spmd} | conditional | flops 1103118336 | bytes 70451288 | solution.py:69
  130.1 2.1 fusion.26
  132.3 4.1 %bitcast_add_fusion.1 = f32[256,4,8,128]{3,0,2,1:T(8,128)S(1)} fusion(f32[256,4,8,128]{3,0,2,1:T(8,128)S(1)} %copy-done.2, f32[256,4,8]{0,2,1:T(8,128)S(1)} %get-tuple-element.500, f32[4,256,256,8]{2,1,3,0:T(8,128)S(1)} %get-tuple-element.508, f32[256,4,8]{0,2,1:T(8,128)S(1)} %max.5, pred[256,256]{0,1:T(8,128)(4,1)S(1)} %get-tuple-element.389, ...), kind=kOutput, calls=%fused_computation.30 | convolution fusion | flops 549453824 | bytes 17170432 | tf_op jit(solution)/shard_map/while/body/eval_jaxpr/while/body/eval_jaxpr/cond/branch_1_fun/tgjk,kgd->tgjd/dot_general | solution.py:58
  136.4 1.9 copy-done.3
  142.1 9.4 %collective-permute-done = bf16[2,256,4,128]{3,1,2,0:T(8,128)(2,1)S(1)} collective-permute-done((bf16[2,256,4,128]{3,1,2,0:T(8,128)(2,1)S(1)}, bf16[2,256,4,128]{3,1,2,0:T(8,128)(2,1)S(1)}, u32[]{:S(2)}, u32[]{:S(2)}) %collective-permute-start) | collective-permute-done | bytes 524320 | tf_op jit(solution)/shard_map/while/body/eval_jaxpr/ppermute | solution.py:17
  151.5 9.6 %conditional.6 = ((f32[256,4,8]{0,2,1:T(8,128)S(1)}, f32[256,4,8]{0,2,1:T(8,128)S(1)}, f32[256,4,8,128]{3,0,2,1:T(8,128)})) conditional(s32[]{:T(128)} %convert_element_type.49, (f32[256,4,8]{0,2,1:T(8,128)S(1)}, f32[256,4,8]{0,2,1:T(8,128)S(1)}, f32[256,4,8,128]{3,0,2,1:T(8,128)}) %tuple.81, (pred[256,256]{0,1:T(8,128)(4,1)S(1)}, ...), branch_computations={%region_7.7_spmd, %region_8.10_spmd} | conditional | flops 1103118336 | bytes 70451288 | solution.py:69
  152.9 2.1 fusion.26
  155.1 4.1 %bitcast_add_fusion.1 = f32[256,4,8,128]{3,0,2,1:T(8,128)S(1)} fusion(f32[256,4,8,128]{3,0,2,1:T(8,128)S(1)} %copy-done.2, f32[256,4,8]{0,2,1:T(8,128)S(1)} %get-tuple-element.500, f32[4,256,256,8]{2,1,3,0:T(8,128)S(1)} %get-tuple-element.508, f32[256,4,8]{0,2,1:T(8,128)S(1)} %max.5, pred[256,256]{0,1:T(8,128)(4,1)S(1)} %get-tuple-element.389, ...), kind=kOutput, calls=%fused_computation.30 | convolution fusion | flops 549453824 | bytes 17170432 | tf_op jit(solution)/shard_map/while/body/eval_jaxpr/while/body/eval_jaxpr/cond/branch_1_fun/tgjk,kgd->tgjd/dot_general | solution.py:58
  159.2 1.9 copy-done.3
  161.2 1.9 collective-permute-start
  164.8 8.7 %collective-permute-done = bf16[2,256,4,128]{3,1,2,0:T(8,128)(2,1)S(1)} collective-permute-done((bf16[2,256,4,128]{3,1,2,0:T(8,128)(2,1)S(1)}, bf16[2,256,4,128]{3,1,2,0:T(8,128)(2,1)S(1)}, u32[]{:S(2)}, u32[]{:S(2)}) %collective-permute-start) | collective-permute-done | bytes 524320 | tf_op jit(solution)/shard_map/while/body/eval_jaxpr/ppermute | solution.py:17
  173.5 9.6 %conditional.6 = ((f32[256,4,8]{0,2,1:T(8,128)S(1)}, f32[256,4,8]{0,2,1:T(8,128)S(1)}, f32[256,4,8,128]{3,0,2,1:T(8,128)})) conditional(s32[]{:T(128)} %convert_element_type.49, (f32[256,4,8]{0,2,1:T(8,128)S(1)}, f32[256,4,8]{0,2,1:T(8,128)S(1)}, f32[256,4,8,128]{3,0,2,1:T(8,128)}) %tuple.81, (pred[256,256]{0,1:T(8,128)(4,1)S(1)}, ...), branch_computations={%region_7.7_spmd, %region_8.10_spmd} | conditional | flops 1103118336 | bytes 70451288 | solution.py:69
  174.9 2.1 fusion.26
  177.1 4.1 %bitcast_add_fusion.1 = f32[256,4,8,128]{3,0,2,1:T(8,128)S(1)} fusion(f32[256,4,8,128]{3,0,2,1:T(8,128)S(1)} %copy-done.2, f32[256,4,8]{0,2,1:T(8,128)S(1)} %get-tuple-element.500, f32[4,256,256,8]{2,1,3,0:T(8,128)S(1)} %get-tuple-element.508, f32[256,4,8]{0,2,1:T(8,128)S(1)} %max.5, pred[256,256]{0,1:T(8,128)(4,1)S(1)} %get-tuple-element.389, ...), kind=kOutput, calls=%fused_computation.30 | convolution fusion | flops 549453824 | bytes 17170432 | tf_op jit(solution)/shard_map/while/body/eval_jaxpr/while/body/eval_jaxpr/cond/branch_1_fun/tgjk,kgd->tgjd/dot_general | solution.py:58
  181.2 1.9 copy-done.3
  183.2 2.9 %divide_convert_fusion = bf16[256,4,8,128]{3,0,2,1:T(8,128)(2,1)S(1)} fusion(f32[256,4,8,128]{3,0,2,1:T(8,128)} %get-tuple-element.416, f32[256,4,8]{0,2,1:T(8,128)S(1)} %get-tuple-element.417), kind=kLoop, calls=%fused_computation.52 | loop fusion | flops 2097152 | bytes 6324224 | tf_op jit(solution)/shard_map/convert_element_type | solution.py:125
  186.1 2.7 %copy.12 = bf16[256,4,8,128]{3,2,1,0:T(8,128)(2,1)} copy(bf16[256,4,8,128]{3,0,2,1:T(8,128)(2,1)S(1)} %divide_convert_fusion) | data formatting | bytes 4194304 | tf_op jit(solution)/shard_map/convert_element_type | solution.py:125
  188.8 2.8 %convert_element_type.36 = bf16[1,256,4096]{2,1,0:T(8,128)(2,1)S(1)} reshape(bf16[256,4,8,128]{3,2,1,0:T(8,128)(2,1)} %copy.12) | data formatting | bytes 4194304 | tf_op jit(solution)/shard_map/convert_element_type | solution.py:125
  193.1 41.3 %collective-permute-done.1 = bf16[1,256,4096]{2,1,0:T(8,128)(2,1)S(1)} collective-permute-done((bf16[1,256,4096]{2,1,0:T(8,128)(2,1)S(1)}, bf16[1,256,4096]{2,1,0:T(8,128)(2,1)S(1)}, u32[]{:S(2)}, u32[]{:S(2)}) %collective-permute-start.1) | collective-permute-done | bytes 2097184 | tf_op jit(solution)/shard_map/ppermute | solution.py:22
  (134 shorter events, 35.8 us)
Async XLA Ops:
  0.0 9.9 %copy-start.5 = (bf16[1,256,4,128]{3,2,1,0:T(4,128)(2,1)S(1)}, bf16[1,256,4,128]{3,2,1,0:T(4,128)(2,1)}, u32[]{:S(2)}) copy-start(bf16[1,256,4,128]{3,2,1,0:T(4,128)(2,1)} %param.12) | copy-start | bytes 786436
  0.0 9.9 %copy-start.4 = (bf16[1,256,4,128]{3,2,1,0:T(4,128)(2,1)S(1)}, bf16[1,256,4,128]{3,2,1,0:T(4,128)(2,1)}, u32[]{:S(2)}) copy-start(bf16[1,256,4,128]{3,2,1,0:T(4,128)(2,1)} %param.11) | copy-start | bytes 786436
  11.4 2.2 copy-start
  17.8 1.9 copy-start.1
  19.7 15.5 %collective-permute-start = (bf16[2,256,4,128]{3,1,2,0:T(8,128)(2,1)S(1)}, bf16[2,256,4,128]{3,1,2,0:T(8,128)(2,1)S(1)}, u32[]{:S(2)}, u32[]{:S(2)}) collective-permute-start(bf16[2,256,4,128]{3,1,2,0:T(8,128)(2,1)S(1)} %get-tuple-element.611), channel_id=1, source_target_pairs={{0,2},{2,4},{4,6},{6,8},{8,10},{10,12},{12,14},{14,16},{16,18},{18... | collective-permute-start | bytes 1572872 | tf_op jit(solution)/shard_map/while/body/eval_jaxpr/ppermute | solution.py:17
  35.3 3.5 %copy-start.2 = (f32[256,4,8,128]{3,0,2,1:T(8,128)S(1)}, f32[256,4,8,128]{3,0,2,1:T(8,128)}, u32[]{:S(2)}) copy-start(f32[256,4,8,128]{3,0,2,1:T(8,128)} %get-tuple-element.393) | copy-start | bytes 12582916 | tf_op jit(solution)/shard_map/while/body/eval_jaxpr/while/body/eval_jaxpr/cond
  43.0 1.9 copy-start.3
  44.9 14.7 %collective-permute-start = (bf16[2,256,4,128]{3,1,2,0:T(8,128)(2,1)S(1)}, bf16[2,256,4,128]{3,1,2,0:T(8,128)(2,1)S(1)}, u32[]{:S(2)}, u32[]{:S(2)}) collective-permute-start(bf16[2,256,4,128]{3,1,2,0:T(8,128)(2,1)S(1)} %get-tuple-element.611), channel_id=1, source_target_pairs={{0,2},{2,4},{4,6},{6,8},{8,10},{10,12},{12,14},{14,16},{16,18},{18... | collective-permute-start | bytes 1572872 | tf_op jit(solution)/shard_map/while/body/eval_jaxpr/ppermute | solution.py:17
  59.6 3.5 %copy-start.2 = (f32[256,4,8,128]{3,0,2,1:T(8,128)S(1)}, f32[256,4,8,128]{3,0,2,1:T(8,128)}, u32[]{:S(2)}) copy-start(f32[256,4,8,128]{3,0,2,1:T(8,128)} %get-tuple-element.393) | copy-start | bytes 12582916 | tf_op jit(solution)/shard_map/while/body/eval_jaxpr/while/body/eval_jaxpr/cond
  67.3 1.9 copy-start.3
  69.3 13.8 %collective-permute-start = (bf16[2,256,4,128]{3,1,2,0:T(8,128)(2,1)S(1)}, bf16[2,256,4,128]{3,1,2,0:T(8,128)(2,1)S(1)}, u32[]{:S(2)}, u32[]{:S(2)}) collective-permute-start(bf16[2,256,4,128]{3,1,2,0:T(8,128)(2,1)S(1)} %get-tuple-element.611), channel_id=1, source_target_pairs={{0,2},{2,4},{4,6},{6,8},{8,10},{10,12},{12,14},{14,16},{16,18},{18... | collective-permute-start | bytes 1572872 | tf_op jit(solution)/shard_map/while/body/eval_jaxpr/ppermute | solution.py:17
  83.1 3.5 %copy-start.2 = (f32[256,4,8,128]{3,0,2,1:T(8,128)S(1)}, f32[256,4,8,128]{3,0,2,1:T(8,128)}, u32[]{:S(2)}) copy-start(f32[256,4,8,128]{3,0,2,1:T(8,128)} %get-tuple-element.393) | copy-start | bytes 12582916 | tf_op jit(solution)/shard_map/while/body/eval_jaxpr/while/body/eval_jaxpr/cond
  90.8 1.9 copy-start.3
  92.8 12.8 %collective-permute-start = (bf16[2,256,4,128]{3,1,2,0:T(8,128)(2,1)S(1)}, bf16[2,256,4,128]{3,1,2,0:T(8,128)(2,1)S(1)}, u32[]{:S(2)}, u32[]{:S(2)}) collective-permute-start(bf16[2,256,4,128]{3,1,2,0:T(8,128)(2,1)S(1)} %get-tuple-element.611), channel_id=1, source_target_pairs={{0,2},{2,4},{4,6},{6,8},{8,10},{10,12},{12,14},{14,16},{16,18},{18... | collective-permute-start | bytes 1572872 | tf_op jit(solution)/shard_map/while/body/eval_jaxpr/ppermute | solution.py:17
  105.6 3.5 %copy-start.2 = (f32[256,4,8,128]{3,0,2,1:T(8,128)S(1)}, f32[256,4,8,128]{3,0,2,1:T(8,128)}, u32[]{:S(2)}) copy-start(f32[256,4,8,128]{3,0,2,1:T(8,128)} %get-tuple-element.393) | copy-start | bytes 12582916 | tf_op jit(solution)/shard_map/while/body/eval_jaxpr/while/body/eval_jaxpr/cond
  113.3 1.9 copy-start.3
  115.3 13.4 %collective-permute-start = (bf16[2,256,4,128]{3,1,2,0:T(8,128)(2,1)S(1)}, bf16[2,256,4,128]{3,1,2,0:T(8,128)(2,1)S(1)}, u32[]{:S(2)}, u32[]{:S(2)}) collective-permute-start(bf16[2,256,4,128]{3,1,2,0:T(8,128)(2,1)S(1)} %get-tuple-element.611), channel_id=1, source_target_pairs={{0,2},{2,4},{4,6},{6,8},{8,10},{10,12},{12,14},{14,16},{16,18},{18... | collective-permute-start | bytes 1572872 | tf_op jit(solution)/shard_map/while/body/eval_jaxpr/ppermute | solution.py:17
  128.7 3.5 %copy-start.2 = (f32[256,4,8,128]{3,0,2,1:T(8,128)S(1)}, f32[256,4,8,128]{3,0,2,1:T(8,128)}, u32[]{:S(2)}) copy-start(f32[256,4,8,128]{3,0,2,1:T(8,128)} %get-tuple-element.393) | copy-start | bytes 12582916 | tf_op jit(solution)/shard_map/while/body/eval_jaxpr/while/body/eval_jaxpr/cond
  136.4 1.9 copy-start.3
  138.4 13.1 %collective-permute-start = (bf16[2,256,4,128]{3,1,2,0:T(8,128)(2,1)S(1)}, bf16[2,256,4,128]{3,1,2,0:T(8,128)(2,1)S(1)}, u32[]{:S(2)}, u32[]{:S(2)}) collective-permute-start(bf16[2,256,4,128]{3,1,2,0:T(8,128)(2,1)S(1)} %get-tuple-element.611), channel_id=1, source_target_pairs={{0,2},{2,4},{4,6},{6,8},{8,10},{10,12},{12,14},{14,16},{16,18},{18... | collective-permute-start | bytes 1572872 | tf_op jit(solution)/shard_map/while/body/eval_jaxpr/ppermute | solution.py:17
  151.5 3.5 %copy-start.2 = (f32[256,4,8,128]{3,0,2,1:T(8,128)S(1)}, f32[256,4,8,128]{3,0,2,1:T(8,128)}, u32[]{:S(2)}) copy-start(f32[256,4,8,128]{3,0,2,1:T(8,128)} %get-tuple-element.393) | copy-start | bytes 12582916 | tf_op jit(solution)/shard_map/while/body/eval_jaxpr/while/body/eval_jaxpr/cond
  159.2 1.9 copy-start.3
  161.2 12.3 %collective-permute-start = (bf16[2,256,4,128]{3,1,2,0:T(8,128)(2,1)S(1)}, bf16[2,256,4,128]{3,1,2,0:T(8,128)(2,1)S(1)}, u32[]{:S(2)}, u32[]{:S(2)}) collective-permute-start(bf16[2,256,4,128]{3,1,2,0:T(8,128)(2,1)S(1)} %get-tuple-element.611), channel_id=1, source_target_pairs={{0,2},{2,4},{4,6},{6,8},{8,10},{10,12},{12,14},{14,16},{16,18},{18... | collective-permute-start | bytes 1572872 | tf_op jit(solution)/shard_map/while/body/eval_jaxpr/ppermute | solution.py:17
  173.5 3.5 %copy-start.2 = (f32[256,4,8,128]{3,0,2,1:T(8,128)S(1)}, f32[256,4,8,128]{3,0,2,1:T(8,128)}, u32[]{:S(2)}) copy-start(f32[256,4,8,128]{3,0,2,1:T(8,128)} %get-tuple-element.393) | copy-start | bytes 12582916 | tf_op jit(solution)/shard_map/while/body/eval_jaxpr/while/body/eval_jaxpr/cond
  181.2 1.9 copy-start.3
  191.6 42.9 %collective-permute-start.1 = (bf16[1,256,4096]{2,1,0:T(8,128)(2,1)S(1)}, bf16[1,256,4096]{2,1,0:T(8,128)(2,1)S(1)}, u32[]{:S(2)}, u32[]{:S(2)}) collective-permute-start(bf16[1,256,4096]{2,1,0:T(8,128)(2,1)S(1)} %convert_element_type.36), channel_id=1, source_target_pairs={{0,64},{64,128},{128,192},{192,0},{1,65},{65,129},{129,193},{193,1... | collective-permute-start | bytes 6291464 | tf_op jit(solution)/shard_map/ppermute | solution.py:22
where the time goes:
time: 236 us
  waiting for transfers between devices  110 us (47%)
  matrix products  43.9 us (19%)
  local copies, waits for them, and re-layouts  32.5 us (14%)
  other arithmetic  27 us (11%)
  starting transfers between devices  16.5 us (7%)
  loops' own time  5.38 us (2%)
    ppermute x7, waiting for transfers between devices, passed_along(): lax.ppermute(value, axis, [(source, source + steps) for source in range(l...  68.5 us
    ppermute x1, waiting for transfers between devices, shifted(): lax.ppermute(shard, axis, [(i, (i + by) % peers) for i in range(peers)])  41.3 us
    dot_general x8, matrix products, update(): jnp.einsum('tgjk,kgd->tgjd', weight.astype(jnp.bfloat16), paired[1], pref...  33.1 us
    reduce_sum x8, other arithmetic, update(): row_total = row_total * factor + jnp.sum(weight, axis=-1)  17.1 us
    cond x40, local copies, waits for them, and re-layouts  15.5 us
    ppermute x7, starting transfers between devices, passed_along(): lax.ppermute(value, axis, [(source, source + steps) for source in range(l...  15 us
    dot_general x8, matrix products, update(): jnp.einsum('tgjd,kgd->tgjk', grouped_heads, paired[0], preferred_element_...  10.8 us
    reduce_or x8, other arithmetic, visit(): return lax.cond(jnp.any(allowed), update, keep, carry)  6.66 us
  transfers between devices with their start and end apart: 8, of which 8 were waited for; matrix products, arithmetic and copies ran while one was open for 3% of the time, Pallas kernels for 0%

commit v1 on v0

v1 whole, which is shorter than its diff:
```python
import functools
import math

import jax
import jax.numpy as jnp
from jax import lax
from jax.experimental import pallas as pl
from jax.experimental.pallas import tpu as pltpu
from jax.sharding import PartitionSpec as P

MESH = pl.DeviceIdType.MESH
MIB = 1 << 20
BLK = 128
TOK = 256
D = 128
GROUPS = 4
WIDTH = 8
HEADS = GROUPS * WIDTH
KEYS = 15 * BLK
TILE = 512
PER_TILE = TILE // BLK
CHUNK = 256
NY = 4
NZ = 8
NX = 4
EARLY = GROUPS - 1
LOW_SCORE = -1e30
SCALE = math.log2(math.e) / math.sqrt(D)


def score_tile(q, km, scores, peaks, causal):
    peak = None
    for c in range(0, KEYS, CHUNK):
        w = min(CHUNK, KEYS - c)
        s = lax.dot_general(
            q, km[c : c + w], (((1,), (1,)), ((), ())), preferred_element_type=jnp.float32
        )
        if c + w == KEYS:
            last = jnp.where(causal, s[:, w - BLK :], LOW_SCORE)
            s = last if w == BLK else jnp.concatenate([s[:, : w - BLK], last], axis=1)
        scores[:, c : c + w] = s
        for b in range(0, w, BLK):
            part = s[:, b : b + BLK]
            peak = part if peak is None else jnp.maximum(peak, part)
    peaks[...] = peak


def mix_tile(scores, peaks, weights, va):
    peak = jnp.max(peaks[...], axis=1, keepdims=True)
    for c in range(0, KEYS, CHUNK):
        w = min(CHUNK, KEYS - c)
        weights[:, c : c + w] = jnp.exp2((scores[:, c : c + w] - peak) * SCALE).astype(jnp.bfloat16)
    mixed = jnp.dot(weights[...], va[...], preferred_element_type=jnp.float32)
    return mixed[:, :D] / mixed[:, D:]


def kernel(
    docs, q_hbm, k_hbm, v_hbm, out_hbm,
    q_in, k_in, v_in, wide, heads, first, kv, km, va,
    scores_a, scores_b, peaks_a, peaks_b, weights_a, weights_b, done,
    in_sem, g_send, g_recv, e_send, e_recv, x_send, x_recv, l_sem,
):
    sec, ctx, tp = lax.axis_index("section"), lax.axis_index("ctx"), lax.axis_index("tp")
    z, y = ctx // NY, ctx % NY
    after, before = (sec + 1) % NX, (sec + NX - 1) % NX

    def at(s, zz, yy):
        return (s, zz * NY + yy, tp)

    load_k = pltpu.make_async_copy(k_hbm, k_in, in_sem.at[0])
    load_v = pltpu.make_async_copy(v_hbm, v_in, in_sem.at[1])
    load_q = pltpu.make_async_copy(q_hbm, q_in, in_sem.at[2])
    load_k.start()
    load_v.start()
    load_q.start()

    barrier = pltpu.get_barrier_semaphore()
    peers = [at(after, z, y), at(before, z, y)]
    peers += [at(sec, z, (y + i) % NY) for i in range(1, NY)]
    peers += [at(sec, (z + i) % NZ, y) for i in (1, 2, NZ - 2, NZ - 1)]
    for peer in peers:
        pl.semaphore_signal(barrier, inc=1, device_id=peer, device_id_type=MESH)

    for i, (load, source) in enumerate(((load_k, k_in), (load_v, v_in))):
        load.wait()
        rows = TOK * GROUPS
        wide[:rows] = source[...].astype(jnp.float32)
        for g in range(GROUPS):
            part = wide[pl.ds(g, TOK, stride=GROUPS), :].astype(jnp.bfloat16)
            if g == EARLY:
                first[i] = part
            else:
                kv[g, 0, i] = part

    pl.semaphore_wait(barrier, len(peers))

    def remote(src, dst, ssem, rsem, peer):
        return pltpu.make_async_remote_copy(
            src_ref=src, dst_ref=dst, send_sem=ssem, recv_sem=rsem,
            device_id=peer, device_id_type=MESH,
        )

    def block_copy(g, src_slot, dst_slot, send_slot, peer):
        return remote(
            kv.at[g, src_slot], kv.at[g, dst_slot], g_send.at[g, send_slot],
            g_recv.at[g, dst_slot], peer,
        )

    def to_z(g, steps):
        return block_copy(g, 0, 4 * steps, steps - 1, at(sec, (z + steps) % NZ, y))

    def to_y(g, src_slot, dst_slot, dy):
        return block_copy(g, src_slot, dst_slot, dst_slot + (1 if dst_slot < 4 else 0), at(sec, z, (y + dy) % NY))

    def z_pairs():
        return ((1, z < NZ - 1), (2, jnp.logical_and(z < NZ - 2, y > 0)))

    def y_own():
        return [(0, dy, dy, y + dy < NY) for dy in range(1, NY)]

    def y_near():
        near = [(4, 4 + dy, dy, jnp.logical_and(z >= 1, y + dy < NY)) for dy in range(1, NY)]
        return near + [(4, dy, dy, jnp.logical_and(z >= 1, y + dy >= NY)) for dy in range(1, NY)]

    def y_far():
        return [(8, 4 + dy, dy, jnp.logical_and(z >= 2, y + dy >= NY)) for dy in range(1, NY)]

    def arrived(g, slot, cond):
        @pl.when(cond)
        def _():
            block_copy(g, slot, slot, 0, at(after, z, y)).wait_recv()

    def direct(g):
        for steps, cond in z_pairs():
            @pl.when(cond)
            def _():
                to_z(g, steps).start()
        for src, dst, dy, cond in y_own():
            @pl.when(cond)
            def _():
                to_y(g, src, dst, dy).start()

    def relay(g):
        arrived(g, 4, z >= 1)
        for src, dst, dy, cond in y_near():
            @pl.when(cond)
            def _():
                to_y(g, src, dst, dy).start()
        arrived(g, 8, jnp.logical_and(z >= 2, y > 0))
        for src, dst, dy, cond in y_far():
            @pl.when(cond)
            def _():
                to_y(g, src, dst, dy).start()

    early_kv = remote(first, kv.at[EARLY, 0], e_send.at[0], e_recv.at[0], at(after, z, y))
    early_q = remote(
        heads.at[pl.ds(EARLY * WIDTH, WIDTH)], heads.at[pl.ds(HEADS, WIDTH)],
        e_send.at[1], e_recv.at[1], at(after, z, y),
    )

    direct(0)
    early_kv.start()
    load_q.wait()
    wide[...] = q_in[...].astype(jnp.float32)
    for h in [*range(EARLY * WIDTH, HEADS), *range(EARLY * WIDTH)]:
        heads[h] = wide[pl.ds(h, TOK, stride=HEADS), :].astype(jnp.bfloat16)
        if h == HEADS - 1:
            early_q.start()
            direct(1)
    relay(0)

    row = lax.broadcasted_iota(jnp.int32, (BLK, BLK), 0)
    col = lax.broadcasted_iota(jnp.int32, (BLK, BLK), 1)
    causal = jnp.concatenate([row >= col] * PER_TILE, axis=0)

    def out_copy(g, r, peer):
        src = done.at[g, pl.ds(r * BLK, BLK)]
        dst = out_hbm.at[pl.ds(r * BLK, BLK), pl.ds(pl.multiple_of(g * WIDTH * D, WIDTH * D), WIDTH * D)]
        if peer is None:
            return pltpu.make_async_copy(src, dst, l_sem.at[r])
        return remote(src, dst, x_send.at[g, r], x_recv.at[g, r], peer)

    def group(g, carry):
        @pl.when(g == 1)
        def _():
            early_kv.wait_recv()

        @pl.when(g < GROUPS - 2)
        def _():
            direct(g + 2)

        @pl.when(g < GROUPS - 1)
        def _():
            relay(g + 1)

        for slot in (1, 2, 3, 5, 6, 7):
            arrived(g, slot, ctx >= slot)

        for r in range(2):
            mine = docs[2 * ctx + r]
            spare = jnp.broadcast_to(kv[g, 0, 0, r * BLK : r * BLK + 16][:1], (BLK, D))
            for b in range(15):
                place = r + b
                slot, half = 7 - place // 2, place % 2
                rows = slice(half * BLK, half * BLK + BLK)
                to = slice(b * BLK, b * BLK + BLK)
                key, value = kv[g, slot, 0, rows], kv[g, slot, 1, rows]
                if b == 14:
                    km[r, to] = key
                    va[r, to, :D] = value
                    va[r, to, D:] = jnp.ones((BLK, D), jnp.bfloat16)
                else:
                    block = 2 * ctx + r - 14 + b
                    ok = jnp.logical_and(block >= 0, docs[jnp.maximum(block, 0)] == mine)
                    ok = jnp.full((BLK, D), ok.astype(jnp.int32)) > 0
                    km[r, to] = jnp.where(ok, key, spare)
                    va[r, to, :D] = jnp.where(ok, value, jnp.zeros_like(value))
                    va[r, to, D:] = jnp.where(ok, 1.0, 0.0).astype(jnp.bfloat16)

        @pl.when(g == EARLY)
        def _():
            early_q.wait_recv()

        base = g * WIDTH + (g // EARLY) * WIDTH

        def queries(r, n):
            return heads[pl.ds(base + n * PER_TILE, PER_TILE), r * BLK : r * BLK + BLK].reshape(TILE, D)

        def put(r, n, mixed):
            for i in range(PER_TILE):
                h = n * PER_TILE + i
                done[g, r * BLK : r * BLK + BLK, h * D : h * D + D] = mixed[
                    i * BLK : i * BLK + BLK
                ].astype(jnp.bfloat16)

        sides = ((scores_a, peaks_a, weights_a), (scores_b, peaks_b, weights_b))
        tiles = [(r, n) for r in range(2) for n in range(WIDTH // PER_TILE)]
        score_tile(queries(0, 0), km.at[0], scores_a, peaks_a, causal)
        for i, (r, n) in enumerate(tiles):
            if i + 1 < len(tiles):
                r1, n1 = tiles[i + 1]
                scores, peaks, _ = sides[(i + 1) % 2]
                score_tile(queries(r1, n1), km.at[r1], scores, peaks, causal)
            scores, peaks, weights = sides[i % 2]
            put(r, n, mix_tile(scores, peaks, weights, va.at[r]))
            if n == WIDTH // PER_TILE - 1:
                @pl.when(g < EARLY)
                def _():
                    out_copy(g, r, at(after, z, y)).start()

                @pl.when(g == EARLY)
                def _():
                    out_copy(g, r, None).start()
        return carry

    lax.fori_loop(0, GROUPS, group, 0)

    early_kv.wait_send()
    early_q.wait_send()
    for r in range(2):
        out_copy(EARLY, r, None).wait()

    def finish(g, carry):
        for steps, cond in z_pairs():
            @pl.when(cond)
            def _():
                to_z(g, steps).wait_send()
        for src, dst, dy, cond in y_own() + y_near() + y_far():
            @pl.when(cond)
            def _():
                to_y(g, src, dst, dy).wait_send()

        @pl.when(g < EARLY)
        def _():
            for r in range(2):
                out_copy(g, r, at(after, z, y)).wait()
        return carry

    lax.fori_loop(0, GROUPS, finish, 0)


def local(queries, key_heads, section_values, block_docs):
    bf16, f32 = jnp.bfloat16, jnp.float32
    anywhere = pl.BlockSpec(memory_space=pl.ANY)
    out = pl.pallas_call(
        kernel,
        out_shape=jax.ShapeDtypeStruct((TOK, HEADS * D), bf16),
        in_specs=[pl.BlockSpec(memory_space=pltpu.SMEM), anywhere, anywhere, anywhere],
        out_specs=anywhere,
        scratch_shapes=[
            pltpu.VMEM((TOK * HEADS, D), bf16),
            pltpu.VMEM((TOK * GROUPS, D), bf16),
            pltpu.VMEM((TOK * GROUPS, D), bf16),
            pltpu.VMEM((TOK * HEADS, D), f32),
            pltpu.VMEM((HEADS + WIDTH, TOK, D), bf16),
            pltpu.VMEM((2, TOK, D), bf16),
            pltpu.VMEM((GROUPS, 9, 2, TOK, D), bf16),
            pltpu.VMEM((2, KEYS, D), bf16),
            pltpu.VMEM((2, KEYS, 2 * D), bf16),
            pltpu.VMEM((TILE, KEYS), f32),
            pltpu.VMEM((TILE, KEYS), f32),
            pltpu.VMEM((TILE, BLK), f32),
            pltpu.VMEM((TILE, BLK), f32),
            pltpu.VMEM((TILE, KEYS), bf16),
            pltpu.VMEM((TILE, KEYS), bf16),
            pltpu.VMEM((GROUPS, TOK, WIDTH * D), bf16),
            pltpu.SemaphoreType.DMA((3,)),
            pltpu.SemaphoreType.DMA((GROUPS, 9)),
            pltpu.SemaphoreType.DMA((GROUPS, 9)),
            pltpu.SemaphoreType.DMA((2,)),
            pltpu.SemaphoreType.DMA((2,)),
            pltpu.SemaphoreType.DMA((GROUPS, 2)),
            pltpu.SemaphoreType.DMA((GROUPS, 2)),
            pltpu.SemaphoreType.DMA((2,)),
        ],
        compiler_params=pltpu.CompilerParams(
            collective_id=0, has_side_effects=True, vmem_limit_bytes=56 * MIB
        ),
    )(
        block_docs,
        queries.reshape(TOK * HEADS, D),
        key_heads.reshape(TOK * GROUPS, D),
        section_values.reshape(TOK * GROUPS, D),
    )
    return out[None]


def solution(mesh):
    specs = P("section", "ctx", "tp", None)
    return jax.shard_map(
        local,
        mesh=mesh,
        in_specs=(specs, specs, specs, P()),
        out_specs=P("section", "ctx", "tp"),
        check_vma=False,
    )
```

time: 236 us -> 76.7 us (0.33)
  waiting for transfers between devices: 110 us -> 0 us
  Pallas kernels: 0 us -> 73.4 us
  matrix products: 43.9 us -> 0 us
  local copies, waits for them, and re-layouts: 32.5 us -> 3.13 us
  other arithmetic: 27 us -> 0 us
  starting transfers between devices: 16.5 us -> 0 us
  loops' own time: 5.38 us -> 0 us
    ppermute x8 -> x0, waiting for transfers between devices: 110 us -> none  [the longest x7 68.5 us: passed_along(): lax.ppermute(value, axis, [(source, source + steps) for source in range(l...]
    pallas_call x0 -> x1, Pallas kernels: none -> 73.4 us  [local(): pl.pallas_call(kernel, out_shape=jax.ShapeDtypeStruct((TOK, HEADS * D), b...]
    dot_general x16 -> x0, matrix products: 43.9 us -> none  [the longest x8 33.1 us: update(): jnp.einsum('tgjk,kgd->tgjd', weight.astype(jnp.bfloat16), paired[1], pref...]
    reduce_sum x8 -> x0, other arithmetic: 17.1 us -> none  [update(): row_total = row_total * factor + jnp.sum(weight, axis=-1)]
    ppermute x8 -> x0, starting transfers between devices: 16.5 us -> none  [the longest x7 15 us: passed_along(): lax.ppermute(value, axis, [(source, source + steps) for source in range(l...]
    cond x40 -> x0, local copies, waits for them, and re-layouts: 15.5 us -> none
    reduce_or x8 -> x0, other arithmetic: 6.66 us -> none  [visit(): return lax.cond(jnp.any(allowed), update, keep, carry)]
    convert_element_type x2 -> x0, local copies, waits for them, and re-layouts: 5.49 us -> none  [local(): attention = (mixture / row_total[..., None]).reshape(count_of_rows, head_...]
  transfers between devices with their start and end apart: 8 -> 0, of which waited for: 8 -> 0; matrix products, arithmetic and copies ran while one was open for 3% -> 0% of each run, Pallas kernels for 0% -> 0%
where the time goes in v1:
time: 76.7 us; the launch traced here: 76.5 us
  Pallas kernels  73.4 us (96%)
  local copies, waits for them, and re-layouts  3.13 us (4%)
    pallas_call x1, Pallas kernels, local(): pl.pallas_call(kernel, out_shape=jax.ShapeDtypeStruct((TOK, HEADS * D), b...  73.4 us
    unnamed x1, local copies, waits for them, and re-layouts  3.13 us

profile of v1, /device:TPU:56, one launch (start us, length us, event | category | flops | bytes accessed | tf_op | source)
XLA Modules:
  0.0 76.5 jit_solution(7703144603548493844)
XLA Ops:
  0.0 73.4 %shard_map.46 = bf16[256,4096]{1,0:T(8,128)(2,1)} custom-call(s32[64]{0:T(128)} %docs.1, bf16[8192,128]{1,0:T(8,128)(2,1)} %bitcast.5, bf16[1024,128]{1,0:T(8,128)(2,1)} %bitcast.6, bf16[1024,128]{1,0:T(8,128)(2,1)} %bitcast.7), custom_call_target="tpu_custom_call" | custom-call | tf_op jit(solution)/shard_map/pallas_call | solution.py:285
  73.4 3.1 %copy.6 = bf16[1,256,4096]{2,1,0:T(8,128)(2,1)} copy(bf16[1,256,4096]{2,1,0:T(8,128)(2,1)} %bitcast.4) | data formatting | bytes 4194304

commit v2 on v1

v2 whole, which is shorter than its diff:
```python
import functools
import math

import jax
import jax.numpy as jnp
from jax import lax
from jax.experimental import pallas as pl
from jax.experimental.pallas import tpu as pltpu
from jax.sharding import PartitionSpec as P

MESH = pl.DeviceIdType.MESH
MIB = 1 << 20
BLK = 128
TOK = 256
D = 128
GROUPS = 4
WIDTH = 8
HEADS = GROUPS * WIDTH
NEAR = 11 * BLK
FAR = 4 * BLK
TILE = 512
PER_TILE = TILE // BLK
CHUNK = 256
NY = 4
NZ = 8
NX = 4
EARLY = 2
LONG = 4
SHORT = WIDTH - LONG
LOW_SCORE = -1e30
SCALE = math.log2(math.e) / math.sqrt(D)


def score_tile(q, km, scores, peaks, causal):
    keys, peak = km.shape[0], None
    for c in range(0, keys, CHUNK):
        w = min(CHUNK, keys - c)
        s = lax.dot_general(
            q, km[c : c + w], (((1,), (1,)), ((), ())), preferred_element_type=jnp.float32
        )
        if causal is not None and c + w == keys:
            last = jnp.where(causal, s[:, w - BLK :], LOW_SCORE)
            s = last if w == BLK else jnp.concatenate([s[:, : w - BLK], last], axis=1)
        scores[:, c : c + w] = s
        for b in range(0, w, BLK):
            part = s[:, b : b + BLK]
            peak = part if peak is None else jnp.maximum(peak, part)
    peaks[...] = peak


def mix_tile(scores, peak, weights, va):
    keys = va.shape[0]
    for c in range(0, keys, CHUNK):
        w = min(CHUNK, keys - c)
        weights[:, c : c + w] = jnp.exp2((scores[:, c : c + w] - peak) * SCALE).astype(jnp.bfloat16)
    return jnp.dot(weights[:, :keys], va[...], preferred_element_type=jnp.float32)


def kernel(
    docs, q_hbm, k_hbm, v_hbm, out_hbm,
    q_in, k_in, v_in, wide, heads, first, kv, km_near, va_near, km_far, va_far,
    scores_a, scores_b, peaks_a, peaks_b, weights_a, weights_b, kept_mix, kept_peak, done, hop_q,
    in_sem, g_send, g_recv, r_send, r_recv, k_send, k_recv, q_send, q_recv, hq_send, hq_recv,
    x_send, x_recv, l_sem,
):
    sec, ctx, tp = lax.axis_index("section"), lax.axis_index("ctx"), lax.axis_index("tp")
    z, y = ctx // NY, ctx % NY
    after, before = (sec + 1) % NX, (sec + NX - 1) % NX

    def at(s, zz, yy):
        return (s, zz * NY + yy, tp)

    load_k = pltpu.make_async_copy(k_hbm, k_in, in_sem.at[0])
    load_v = pltpu.make_async_copy(v_hbm, v_in, in_sem.at[1])
    load_q = pltpu.make_async_copy(q_hbm, q_in, in_sem.at[2])
    load_k.start()
    load_v.start()
    load_q.start()

    barrier = pltpu.get_barrier_semaphore()
    peers = [at(after, z, y), at(before, z, y)]
    peers += [at(sec, z, (y + i) % NY) for i in (1, NY - 1)]
    peers += [at(sec, (z + i) % NZ, y) for i in (1, NZ - 1)]
    for peer in peers:
        pl.semaphore_signal(barrier, inc=1, device_id=peer, device_id_type=MESH)

    for i, (load, source) in enumerate(((load_k, k_in), (load_v, v_in))):
        load.wait()
        rows = TOK * GROUPS
        wide[:rows] = source[...].astype(jnp.float32)
        for g in range(GROUPS):
            part = wide[pl.ds(g, TOK, stride=GROUPS), :].astype(jnp.bfloat16)
            if g < EARLY:
                kv[g, 0, i] = part
            else:
                first[g - EARLY, i] = part

    pl.semaphore_wait(barrier, len(peers))

    def remote(src, dst, ssem, rsem, peer):
        return pltpu.make_async_remote_copy(
            src_ref=src, dst_ref=dst, send_sem=ssem, recv_sem=rsem,
            device_id=peer, device_id_type=MESH,
        )

    def block_copy(g, src_slot, dst_slot, send_slot, peer):
        return remote(
            kv.at[g, src_slot], kv.at[g, dst_slot], g_send.at[g, send_slot],
            g_recv.at[g, dst_slot], peer,
        )

    def to_z(g, src_slot):
        return block_copy(g, src_slot, src_slot + 4, src_slot // 4, at(sec, (z + 1) % NZ, y))

    def to_y(g, src_slot, dst_slot, dy):
        return block_copy(g, src_slot, dst_slot, dst_slot + (1 if dst_slot < 4 else 0), at(sec, z, (y + dy) % NY))

    def z_pairs():
        onward = jnp.logical_and(z >= 1, jnp.logical_and(z < NZ - 1, y > 0))
        return ((0, z < NZ - 1), (4, onward))

    def y_own():
        return [(0, dy, dy, y + dy < NY) for dy in (1, NY - 1)]

    def y_near():
        near = [(4, 4 + dy, dy, jnp.logical_and(z >= 1, y + dy < NY)) for dy in (1, NY - 1)]
        return near + [(4, dy, dy, jnp.logical_and(z >= 1, y + dy >= NY)) for dy in (1, NY - 1)]

    def y_far():
        return [(8, 4 + dy, dy, jnp.logical_and(z >= 2, y + dy >= NY)) for dy in (1, NY - 1)]

    def arrived(g, slot, cond):
        @pl.when(cond)
        def _():
            block_copy(g, slot, slot, 0, at(after, z, y)).wait_recv()

    def send_z(g, which):
        src, cond = z_pairs()[which]

        @pl.when(cond)
        def _():
            to_z(g, src).start()

    def send_y(g, which):
        for src, dst, dy, cond in which:
            @pl.when(cond)
            def _():
                to_y(g, src, dst, dy).start()

    def send_own(g):
        send_y(g, y_own())

    def send_near(g):
        arrived(g, 4, z >= 1)
        send_z(g, 1)
        send_y(g, y_near())

    def send_far(g):
        arrived(g, 8, jnp.logical_and(z >= 2, y > 0))
        send_y(g, y_far())

    passes = (
        (0, 0, 5, 6, 1, 2), (0, 0, 1, 2, 1, 1), (0, 0, 3, 6, -1, 1), (0, 1, 3, 6, -1, 1),
        (1, 0, 1, 2, 1, 0), (1, 0, 7, 6, -1, 2), (1, 1, 7, 6, -1, 2), (1, 0, 5, 6, 1, 1),
        (2, 0, 1, 2, 1, 0), (2, 1, 1, 2, 1, 0), (2, 1, 7, 6, -1, 2), (2, 1, 3, 2, -1, 1),
        (3, 1, 3, 2, -1, 0), (3, 1, 7, 6, -1, 1), (3, 0, 5, 2, 1, 1), (3, 1, 5, 2, 1, 1),
    )

    def pass_copy(g, part, here, there, dy):
        return remote(
            kv.at[g, here, part], kv.at[g, there, part], r_send.at[g, there // 4, part],
            r_recv.at[g, there // 4, part], at(sec, z, (y + NY + dy) % NY),
        )

    def each_pass(g, act):
        for i in range(4):
            for who, part, here, there, dy, least in passes[i::4]:
                @pl.when(jnp.logical_and(y == who, z >= least))
                def _():
                    act(pass_copy(g, part, here, there, dy))

    def relay_again(g):
        for slot in (1, 3, 5, 7):
            arrived(g, slot, ctx >= slot)
        each_pass(g, lambda copy: copy.start())

    def gathered(g):
        for slot in (2, 6):
            @pl.when(ctx >= slot)
            def _():
                for part in range(2):
                    pass_copy(g, part, slot, slot, 1).wait_recv()

    def early_kv(g):
        return remote(
            first.at[g - EARLY], kv.at[g, 0], k_send.at[g - EARLY], k_recv.at[g - EARLY],
            at(after, z, y),
        )

    moved = EARLY * WIDTH

    def early_q(g):
        return remote(
            heads.at[pl.ds(g * WIDTH, SHORT)], heads.at[pl.ds(g * WIDTH + moved, SHORT)],
            q_send.at[g - EARLY], q_recv.at[g - EARLY], at(after, z, y),
        )

    def long_q(g, step):
        i, own = g - EARLY, g * WIDTH + SHORT
        src = heads.at[pl.ds(own, LONG)] if step == 0 else hop_q.at[i, step - 1]
        dst = heads.at[pl.ds(own + moved, LONG)] if step == 2 else hop_q.at[i, step]
        return remote(src, dst, hq_send.at[i, step], hq_recv.at[i, step], at(before, z, y))

    def pass_q(g, step):
        long_q(g, step - 1).wait_recv()
        long_q(g, step).start()

    early = range(EARLY, GROUPS)
    send_z(0, 0)
    send_own(0)
    send_z(1, 0)
    for g in early:
        early_kv(g).start()
    load_q.wait()
    wide[...] = q_in[...].astype(jnp.float32)
    for h in [*range(moved, HEADS), *range(moved)]:
        heads[h] = wide[pl.ds(h, TOK, stride=HEADS), :].astype(jnp.bfloat16)
        if h >= moved and (h + 1) % WIDTH == 0:
            early_q(h // WIDTH).start()
            long_q(h // WIDTH, 0).start()
    send_near(0)
    send_own(1)
    send_far(0)
    early_kv(2).wait_recv()
    send_z(2, 0)
    early_kv(3).wait_recv()
    send_z(3, 0)
    pass_q(2, 1)

    row = lax.broadcasted_iota(jnp.int32, (BLK, BLK), 0)
    col = lax.broadcasted_iota(jnp.int32, (BLK, BLK), 1)
    causal = jnp.concatenate([row >= col] * PER_TILE, axis=0)

    def out_copy(g, r, peer):
        src = done.at[g, pl.ds(r * BLK, BLK)]
        dst = out_hbm.at[pl.ds(r * BLK, BLK), pl.ds(pl.multiple_of(g * WIDTH * D, WIDTH * D), WIDTH * D)]
        if peer is None:
            return pltpu.make_async_copy(src, dst, l_sem.at[g, r])
        return remote(src, dst, x_send.at[g, r], x_recv.at[g, r], peer)

    def fill(g, r, blocks, km, va):
        mine = docs[2 * ctx + r]
        spare = jnp.broadcast_to(kv[g, 0, 0, r * BLK : r * BLK + 16][:1], (BLK, D))
        for b, (slot, half) in enumerate(blocks):
            rows = slice(half * BLK, half * BLK + BLK)
            to = slice(b * BLK, b * BLK + BLK)
            key, value = kv[g, slot, 0, rows], kv[g, slot, 1, rows]
            if slot == 0 and half == r:
                km[r, to] = key
                va[r, to, :D] = value
                va[r, to, D:] = jnp.ones((BLK, D), jnp.bfloat16)
            else:
                block = 2 * (ctx - slot) + half
                ok = jnp.logical_and(block >= 0, docs[jnp.maximum(block, 0)] == mine)
                ok = jnp.full((BLK, D), ok.astype(jnp.int32)) > 0
                km[r, to] = jnp.where(ok, key, spare)
                va[r, to, :D] = jnp.where(ok, value, jnp.zeros_like(value))
                va[r, to, D:] = jnp.where(ok, 1.0, 0.0).astype(jnp.bfloat16)

    near_blocks = [(slot, half) for slot in (1, 3, 4, 5) for half in range(2)]
    near_of = (
        near_blocks + [(7, 0), (7, 1), (0, 0)],
        near_blocks + [(7, 1), (0, 0), (0, 1)],
    )
    far_blocks = [(slot, half) for slot in (2, 6) for half in range(2)]
    sides = ((scores_a, peaks_a, weights_a), (scores_b, peaks_b, weights_b))
    tiles = [(r, n) for r in range(2) for n in range(WIDTH // PER_TILE)]

    def group(g, carry):
        for slot in (1, 3, 5, 7):
            arrived(g, slot, ctx >= slot)
        each_pass(g, lambda copy: copy.start())

        @pl.when(g < GROUPS - 1)
        def _():
            send_near(g + 1)

        @pl.when(g < GROUPS - 2)
        def _():
            send_own(g + 2)

        @pl.when(g == 1)
        def _():
            pass_q(2, 2)

        @pl.when(g == 2)
        def _():
            pass_q(3, 2)

        for r in range(2):
            fill(g, r, near_of[r], km_near, va_near)

        @pl.when(g == EARLY)
        def _():
            early_q(EARLY).wait_recv()
            long_q(EARLY, 2).wait_recv()

        @pl.when(g == EARLY + 1)
        def _():
            early_q(EARLY + 1).wait_recv()
            long_q(EARLY + 1, 2).wait_recv()

        base = g * WIDTH + (g // EARLY) * moved

        def queries(r, n):
            return heads[pl.ds(base + n * PER_TILE, PER_TILE), r * BLK : r * BLK + BLK].reshape(TILE, D)

        def score(i, km, mask):
            r, n = tiles[i]
            scores, peaks, _ = sides[i % 2]
            score_tile(queries(r, n), km.at[r], scores, peaks, mask)

        score(0, km_near, causal)
        for i, (r, n) in enumerate(tiles):
            if i + 1 < len(tiles):
                score(i + 1, km_near, causal)
            scores, peaks, weights = sides[i % 2]
            peak = jnp.max(peaks[...], axis=1, keepdims=True)
            kept_peak[i] = jnp.broadcast_to(peak, (TILE, D))
            kept_mix[i] = mix_tile(scores, peak, weights, va_near.at[r])
            if i == 1:
                @pl.when(g < GROUPS - 1)
                def _():
                    send_far(g + 1)

                @pl.when(g == 0)
                def _():
                    pass_q(3, 1)

        gathered(g)
        for r in range(2):
            fill(g, r, far_blocks, km_far, va_far)

        score(0, km_far, None)
        for i, (r, n) in enumerate(tiles):
            if i + 1 < len(tiles):
                score(i + 1, km_far, None)
            scores, peaks, weights = sides[i % 2]
            old = kept_peak[i][:, :1]
            peak = jnp.maximum(old, jnp.max(peaks[...], axis=1, keepdims=True))
            mixed = mix_tile(scores, peak, weights, va_far.at[r])
            mixed = mixed + kept_mix[i] * jnp.exp2((old - peak) * SCALE)
            mixed = (mixed[:, :D] / mixed[:, D:]).astype(jnp.bfloat16)
            for j in range(PER_TILE):
                h = n * PER_TILE + j
                done[g, r * BLK : r * BLK + BLK, h * D : h * D + D] = mixed[j * BLK : j * BLK + BLK]
            if n == WIDTH // PER_TILE - 1:
                @pl.when(g < EARLY)
                def _():
                    out_copy(g, r, at(after, z, y)).start()

                @pl.when(g >= EARLY)
                def _():
                    out_copy(g, r, None).start()
        return carry

    lax.fori_loop(0, GROUPS, group, 0)

    for g in early:
        early_kv(g).wait_send()
        early_q(g).wait_send()
        for step in range(3):
            long_q(g, step).wait_send()
        for r in range(2):
            out_copy(g, r, None).wait()
    for g in range(EARLY):
        for r in range(2):
            out_copy(g, r, at(after, z, y)).wait()

    def finish(g, carry):
        for src, cond in z_pairs():
            @pl.when(cond)
            def _():
                to_z(g, src).wait_send()
        for src, dst, dy, cond in y_own() + y_near() + y_far():
            @pl.when(cond)
            def _():
                to_y(g, src, dst, dy).wait_send()
        each_pass(g, lambda copy: copy.wait_send())
        return carry

    lax.fori_loop(0, GROUPS, finish, 0)


def local(queries, key_heads, section_values, block_docs):
    bf16, f32 = jnp.bfloat16, jnp.float32
    anywhere = pl.BlockSpec(memory_space=pl.ANY)
    late = GROUPS - EARLY
    dma = pltpu.SemaphoreType.DMA
    out = pl.pallas_call(
        kernel,
        out_shape=jax.ShapeDtypeStruct((TOK, HEADS * D), bf16),
        in_specs=[pl.BlockSpec(memory_space=pltpu.SMEM), anywhere, anywhere, anywhere],
        out_specs=anywhere,
        scratch_shapes=[
            pltpu.VMEM((TOK * HEADS, D), bf16),
            pltpu.VMEM((TOK * GROUPS, D), bf16),
            pltpu.VMEM((TOK * GROUPS, D), bf16),
            pltpu.VMEM((TOK * HEADS, D), f32),
            pltpu.VMEM((HEADS + late * WIDTH, TOK, D), bf16),
            pltpu.VMEM((late, 2, TOK, D), bf16),
            pltpu.VMEM((GROUPS, 9, 2, TOK, D), bf16),
            pltpu.VMEM((2, NEAR, D), bf16),
            pltpu.VMEM((2, NEAR, 2 * D), bf16),
            pltpu.VMEM((2, FAR, D), bf16),
            pltpu.VMEM((2, FAR, 2 * D), bf16),
            pltpu.VMEM((TILE, NEAR), f32),
            pltpu.VMEM((TILE, NEAR), f32),
            pltpu.VMEM((TILE, BLK), f32),
            pltpu.VMEM((TILE, BLK), f32),
            pltpu.VMEM((TILE, NEAR), bf16),
            pltpu.VMEM((TILE, NEAR), bf16),
            pltpu.VMEM((4, TILE, 2 * D), f32),
            pltpu.VMEM((4, TILE, D), f32),
            pltpu.VMEM((GROUPS, TOK, WIDTH * D), bf16),
            pltpu.VMEM((late, 2, LONG, TOK, D), bf16),
            dma((3,)),
            dma((GROUPS, 9)),
            dma((GROUPS, 9)),
            dma((GROUPS, 2, 2)),
            dma((GROUPS, 2, 2)),
            dma((late,)),
            dma((late,)),
            dma((late,)),
            dma((late,)),
            dma((late, 3)),
            dma((late, 3)),
            dma((EARLY, 2)),
            dma((EARLY, 2)),
            dma((GROUPS, 2)),
        ],
        compiler_params=pltpu.CompilerParams(
            collective_id=0, has_side_effects=True, vmem_limit_bytes=56 * MIB
        ),
    )(
        block_docs,
        queries.reshape(TOK * HEADS, D),
        key_heads.reshape(TOK * GROUPS, D),
        section_values.reshape(TOK * GROUPS, D),
    )
    return out[None]


def solution(mesh):
    specs = P("section", "ctx", "tp", None)
    return jax.shard_map(
        local,
        mesh=mesh,
        in_specs=(specs, specs, specs, P()),
        out_specs=P("section", "ctx", "tp"),
        check_vma=False,
    )
```

time: 76.7 us -> 62.5 us (0.81)
  the two profiles are of different devices: /device:TPU:56 before, /device:TPU:70 now
where the time goes in v2:
time: 62.5 us; the launch traced here: 62.4 us
  Pallas kernels  59.3 us (95%)
  local copies, waits for them, and re-layouts  3.13 us (5%)
    pallas_call x1, Pallas kernels, local(): pl.pallas_call(kernel, out_shape=jax.ShapeDtypeStruct((TOK, HEADS * D), b...  59.3 us
    unnamed x1, local copies, waits for them, and re-layouts  3.13 us

profile of v2, /device:TPU:70, one launch (start us, length us, event | category | flops | bytes accessed | tf_op | source)
XLA Modules:
  0.0 62.4 jit_solution(1110628085883530343)
XLA Ops:
  0.0 59.3 %shard_map.46 = bf16[256,4096]{1,0:T(8,128)(2,1)} custom-call(s32[64]{0:T(128)} %docs.1, bf16[8192,128]{1,0:T(8,128)(2,1)} %bitcast.5, bf16[1024,128]{1,0:T(8,128)(2,1)} %bitcast.6, bf16[1024,128]{1,0:T(8,128)(2,1)} %bitcast.7), custom_call_target="tpu_custom_call" | custom-call | tf_op jit(solution)/shard_map/pallas_call | solution.py:400
  59.3 3.1 %copy.6 = bf16[1,256,4096]{2,1,0:T(8,128)(2,1)} copy(bf16[1,256,4096]{2,1,0:T(8,128)(2,1)} %bitcast.4) | data formatting | bytes 4194304

commit v3 on v2

v3 whole, which is shorter than its diff:
```python
import functools
import math

import jax
import jax.numpy as jnp
from jax import lax
from jax.experimental import pallas as pl
from jax.experimental.pallas import tpu as pltpu
from jax.sharding import PartitionSpec as P

MESH = pl.DeviceIdType.MESH
MIB = 1 << 20
BLK = 128
TOK = 256
D = 128
GROUPS = 4
WIDTH = 8
HEADS = GROUPS * WIDTH
NEAR = 11 * BLK
FAR = 4 * BLK
TILE = 1024
PER_TILE = TILE // BLK
CHUNK = 256
NY = 4
NZ = 8
NX = 4
EARLY = 2
LONG = 2
SHORT = WIDTH - LONG
LOW_SCORE = -1e30
SCALE = math.log2(math.e) / math.sqrt(D)


def score_tile(q, pieces, scores, peaks, causal):
    peak, c = None, 0
    for i, (keys, added) in enumerate(pieces):
        s = lax.dot_general(
            q, keys, (((1,), (1,)), ((), ())), preferred_element_type=jnp.float32
        )
        for b, bias in enumerate(added):
            part = s[:, b * BLK : b * BLK + BLK]
            if causal is not None and i + 1 == len(pieces) and b + 1 == len(added):
                part = jnp.where(causal, part, LOW_SCORE)
            else:
                part = part + bias
            scores[:, c : c + BLK] = part
            peak = part if peak is None else jnp.maximum(peak, part)
            c += BLK
    peaks[...] = peak


def mix_tile(scores, peaks, weights, va):
    keys = va.shape[0]
    for t in range(0, TILE, BLK):
        rows = slice(t, t + BLK)
        peak = peaks[rows]
        for c in range(0, keys, BLK):
            part = jnp.exp2((scores[rows, c : c + BLK] - peak) * SCALE)
            weights[rows, c : c + BLK] = part.astype(jnp.bfloat16)
    return jnp.dot(weights[:, :keys], va[...], preferred_element_type=jnp.float32)


def kernel(
    docs, q_hbm, k_hbm, v_hbm, out_hbm,
    q_in, k_in, v_in, wide, heads, first, kv, va_near, va_far,
    scores_a, scores_b, peaks_a, peaks_b, weights_a, weights_b, kept_mix, kept_peak, far_mix, done, hop_q, hop_o,
    in_sem, g_send, g_recv, r_send, r_recv, k_send, k_recv, q_send, q_recv, hq_send, hq_recv,
    ho_send, ho_recv, x_send, x_recv, l_sem,
):
    sec, ctx, tp = lax.axis_index("section"), lax.axis_index("ctx"), lax.axis_index("tp")
    z, y = ctx // NY, ctx % NY
    after, before = (sec + 1) % NX, (sec + NX - 1) % NX

    def at(s, zz, yy):
        return (s, zz * NY + yy, tp)

    load_k = pltpu.make_async_copy(k_hbm, k_in, in_sem.at[0])
    load_v = pltpu.make_async_copy(v_hbm, v_in, in_sem.at[1])
    load_q = pltpu.make_async_copy(q_hbm, q_in, in_sem.at[2])
    load_k.start()
    load_v.start()
    load_q.start()

    barrier = pltpu.get_barrier_semaphore()
    peers = [at(after, z, y), at(before, z, y)]
    peers += [at(sec, z, (y + i) % NY) for i in (1, NY - 1)]
    peers += [at(sec, (z + i) % NZ, y) for i in (1, NZ - 1)]
    for peer in peers:
        pl.semaphore_signal(barrier, inc=1, device_id=peer, device_id_type=MESH)

    for i, (load, source) in enumerate(((load_k, k_in), (load_v, v_in))):
        load.wait()
        rows = TOK * GROUPS
        wide[:rows] = source[...].astype(jnp.float32)
        for g in range(GROUPS):
            part = wide[pl.ds(g, TOK, stride=GROUPS), :].astype(jnp.bfloat16)
            if g < EARLY:
                kv[g, 0, i] = part
            else:
                first[g - EARLY, i] = part

    pl.semaphore_wait(barrier, len(peers))

    def remote(src, dst, ssem, rsem, peer):
        return pltpu.make_async_remote_copy(
            src_ref=src, dst_ref=dst, send_sem=ssem, recv_sem=rsem,
            device_id=peer, device_id_type=MESH,
        )

    def block_copy(g, src_slot, dst_slot, send_slot, peer):
        return remote(
            kv.at[g, src_slot], kv.at[g, dst_slot], g_send.at[g, send_slot],
            g_recv.at[g, dst_slot], peer,
        )

    def to_z(g, src_slot):
        return block_copy(g, src_slot, src_slot + 4, src_slot // 4, at(sec, (z + 1) % NZ, y))

    def to_y(g, src_slot, dst_slot, dy):
        return block_copy(g, src_slot, dst_slot, dst_slot + (1 if dst_slot < 4 else 0), at(sec, z, (y + dy) % NY))

    def z_pairs():
        onward = jnp.logical_and(z >= 1, jnp.logical_and(z < NZ - 1, y > 0))
        return ((0, z < NZ - 1), (4, onward))

    def y_own():
        return [(0, dy, dy, y + dy < NY) for dy in (1, NY - 1)]

    def y_near():
        near = [(4, 4 + dy, dy, jnp.logical_and(z >= 1, y + dy < NY)) for dy in (1, NY - 1)]
        return near + [(4, dy, dy, jnp.logical_and(z >= 1, y + dy >= NY)) for dy in (1, NY - 1)]

    def y_far():
        return [(8, 4 + dy, dy, jnp.logical_and(z >= 2, y + dy >= NY)) for dy in (1, NY - 1)]

    def arrived(g, slot, cond):
        @pl.when(cond)
        def _():
            block_copy(g, slot, slot, 0, at(after, z, y)).wait_recv()

    def send_z(g, which):
        src, cond = z_pairs()[which]

        @pl.when(cond)
        def _():
            to_z(g, src).start()

    def send_y(g, which):
        for src, dst, dy, cond in which:
            @pl.when(cond)
            def _():
                to_y(g, src, dst, dy).start()

    def send_own(g):
        send_y(g, y_own())

    def send_near(g):
        arrived(g, 4, z >= 1)
        send_z(g, 1)
        send_y(g, y_near())

    def send_far(g):
        arrived(g, 8, jnp.logical_and(z >= 2, y > 0))
        send_y(g, y_far())

    passes = (
        (0, 0, 5, 6, 1, 2), (0, 0, 1, 2, 1, 1), (0, 0, 3, 6, -1, 1), (0, 1, 3, 6, -1, 1),
        (1, 0, 1, 2, 1, 0), (1, 0, 7, 6, -1, 2), (1, 1, 7, 6, -1, 2), (1, 0, 5, 6, 1, 1),
        (2, 0, 1, 2, 1, 0), (2, 1, 1, 2, 1, 0), (2, 1, 7, 6, -1, 2), (2, 1, 3, 2, -1, 1),
        (3, 1, 3, 2, -1, 0), (3, 1, 7, 6, -1, 1), (3, 0, 5, 2, 1, 1), (3, 1, 5, 2, 1, 1),
    )

    def pass_copy(g, part, here, there, dy):
        return remote(
            kv.at[g, here, part], kv.at[g, there, part], r_send.at[g, there // 4, part],
            r_recv.at[g, there // 4, part], at(sec, z, (y + NY + dy) % NY),
        )

    def each_pass(g, act):
        for i in range(4):
            for who, part, here, there, dy, least in passes[i::4]:
                @pl.when(jnp.logical_and(y == who, z >= least))
                def _():
                    act(pass_copy(g, part, here, there, dy))

    def relay_again(g):
        for slot in (1, 3, 5, 7):
            arrived(g, slot, ctx >= slot)
        each_pass(g, lambda copy: copy.start())

    def gathered(g):
        for slot in (2, 6):
            @pl.when(ctx >= slot)
            def _():
                for part in range(2):
                    pass_copy(g, part, slot, slot, 1).wait_recv()

    def early_kv(g):
        return remote(
            first.at[g - EARLY], kv.at[g, 0], k_send.at[g - EARLY], k_recv.at[g - EARLY],
            at(after, z, y),
        )

    moved = EARLY * WIDTH

    def early_q(g):
        count = WIDTH if g == EARLY else SHORT
        return remote(
            heads.at[pl.ds(g * WIDTH, count)], heads.at[pl.ds(g * WIDTH + moved, count)],
            q_send.at[g - EARLY], q_recv.at[g - EARLY], at(after, z, y),
        )

    def long_q(step):
        own = (GROUPS - 1) * WIDTH + SHORT
        src = heads.at[pl.ds(own, LONG)] if step == 0 else hop_q.at[step - 1]
        dst = heads.at[pl.ds(own + moved, LONG)] if step == 2 else hop_q.at[step]
        return remote(src, dst, hq_send.at[step], hq_recv.at[step], at(before, z, y))

    def long_out(g, step):
        cols = pl.ds(SHORT * D, LONG * D)
        far_cols = pl.ds(pl.multiple_of(g * WIDTH * D + SHORT * D, LONG * D), LONG * D)
        src = done.at[g, :, cols] if step == 0 else hop_o.at[g, step - 1]
        dst = out_hbm.at[:, far_cols] if step == 2 else hop_o.at[g, step]
        return remote(src, dst, ho_send.at[g, step], ho_recv.at[g, step], at(before, z, y))

    def pass_q(step):
        long_q(step - 1).wait_recv()
        long_q(step).start()

    def pass_out(g, step):
        long_out(g, step - 1).wait_recv()
        long_out(g, step).start()

    early = range(EARLY, GROUPS)
    send_z(0, 0)
    send_own(0)
    send_z(1, 0)
    for g in early:
        early_kv(g).start()
    load_q.wait()
    wide[...] = q_in[...].astype(jnp.float32)
    for h in [*range(moved, HEADS), *range(moved)]:
        heads[h] = wide[pl.ds(h, TOK, stride=HEADS), :].astype(jnp.bfloat16)
        if h >= moved and (h + 1) % WIDTH == 0:
            early_q(h // WIDTH).start()
        if h == HEADS - 1:
            long_q(0).start()
    va_near[:, D:] = jnp.ones((NEAR + BLK, D), jnp.bfloat16)
    va_far[:, D:] = jnp.ones((FAR, D), jnp.bfloat16)
    for slot in range(1, 8):
        @pl.when(ctx < slot)
        def _():
            for g in range(GROUPS):
                kv[g, slot] = jnp.zeros((2, TOK, D), jnp.bfloat16)

    send_near(0)
    send_own(1)
    send_near(1)
    early_kv(2).wait_recv()
    send_z(2, 0)
    early_kv(3).wait_recv()
    send_z(3, 0)
    send_far(0)
    pass_q(1)
    send_far(1)

    row = lax.broadcasted_iota(jnp.int32, (BLK, BLK), 0)
    col = lax.broadcasted_iota(jnp.int32, (BLK, BLK), 1)
    causal = jnp.concatenate([row >= col] * PER_TILE, axis=0)

    def out_copy(g, r, peer):
        width = WIDTH * D if peer is None else SHORT * D
        src = done.at[g, pl.ds(r * BLK, BLK), pl.ds(0, width)]
        dst = out_hbm.at[pl.ds(r * BLK, BLK), pl.ds(pl.multiple_of(g * WIDTH * D, WIDTH * D), width)]
        if peer is None:
            return pltpu.make_async_copy(src, dst, l_sem.at[g, r])
        return remote(src, dst, x_send.at[g, r], x_recv.at[g, r], peer)

    near_slots, far_slots = (7, 1, 3, 4, 5, 0), (2, 6)

    def bring(g, slots, va):
        for i, slot in enumerate(slots):
            va[i * TOK : i * TOK + TOK, :D] = kv[g, slot, 1]

    def pieces_of(g, r, slots):
        mine = docs[2 * ctx + r]
        pieces = []
        for slot in slots:
            halves = (0,) if (slot, r) == (0, 0) else (1,) if (slot, r) == (7, 1) else (0, 1)
            keys = kv[g, slot, 0, halves[0] * BLK : halves[-1] * BLK + BLK]
            added = []
            for half in halves:
                block = 2 * (ctx - slot) + half
                ok = jnp.logical_and(block >= 0, docs[jnp.maximum(block, 0)] == mine)
                added.append(jnp.where(ok, 0.0, LOW_SCORE).astype(jnp.float32))
            pieces.append((keys, added))
        return pieces

    def va_of(r):
        return va_near.at[r * BLK : r * BLK + NEAR]

    sides = ((scores_a, peaks_a, weights_a), (scores_b, peaks_b, weights_b))

    def score(g, r, slots, mask):
        base = g * WIDTH + (g // EARLY) * moved
        q = heads[pl.ds(base, WIDTH), r * BLK : r * BLK + BLK].reshape(TILE, D)
        scores, peaks, _ = sides[r]
        score_tile(q, pieces_of(g, r, slots), scores, peaks, mask)

    def near_part(i, p):
        g = EARLY * p + i

        @pl.when(g == 2)
        def _():
            send_far(3)

        for slot in (1, 3, 5, 7):
            arrived(g, slot, ctx >= slot)
        each_pass(g, lambda copy: copy.start())

        @pl.when(g == 0)
        def _():
            send_near(2)
            send_own(2)
            pass_q(2)

        @pl.when(g == 2)
        def _():
            early_q(2).wait_recv()

        @pl.when(g == 3)
        def _():
            pass_out(1, 1)
            early_q(3).wait_recv()
            long_q(2).wait_recv()

        bring(g, near_slots, va_near)

        score(g, 0, near_slots, causal)
        for r in range(2):
            if r == 0:
                score(g, 1, near_slots, causal)
            scores, peaks, weights = sides[r]
            for t in range(0, TILE, BLK):
                rows = slice(t, t + BLK)
                peak = jnp.max(peaks[rows], axis=1, keepdims=True)
                kept_peak[i, r, rows] = jnp.broadcast_to(peak, (BLK, BLK))
            kept_mix[i, r] = mix_tile(scores, kept_peak.at[i, r], weights, va_of(r))
            if r == 0:
                @pl.when(g == 1)
                def _():
                    send_far(2)
                    send_near(3)
                    send_own(3)

                @pl.when(g == 2)
                def _():
                    pass_out(0, 1)

                @pl.when(g == 3)
                def _():
                    pass_out(0, 2)
        return p

    def far_part(i, p):
        g = EARLY * p + i

        @pl.when(g == 2)
        def _():
            pass_out(1, 2)

        gathered(g)
        bring(g, far_slots, va_far)

        score(g, 0, far_slots, None)
        for r in range(2):
            if r == 0:
                score(g, 1, far_slots, None)
            scores, peaks, weights = sides[r]
            for t in range(0, TILE, BLK):
                rows = slice(t, t + BLK)
                peak = jnp.max(peaks[rows], axis=1, keepdims=True)
                peaks[rows] = jnp.maximum(kept_peak[i, r, rows], peak)
            far_mix[...] = mix_tile(scores, peaks, weights, va_far)
            for h in range(WIDTH):
                rows = slice(h * BLK, h * BLK + BLK)
                factor = jnp.exp2((kept_peak[i, r, rows] - peaks[rows]) * SCALE)
                mixed = far_mix[rows, :D] + kept_mix[i, r, rows, :D] * factor
                total = far_mix[rows, D:] + kept_mix[i, r, rows, D:] * factor
                done[g, r * BLK : r * BLK + BLK, h * D : h * D + D] = (mixed / total).astype(jnp.bfloat16)

            @pl.when(g < EARLY)
            def _():
                out_copy(g, r, at(after, z, y)).start()
                if r == 1:
                    long_out(g, 0).start()

            @pl.when(g >= EARLY)
            def _():
                out_copy(g, r, None).start()
        return p

    def pair(p, carry):
        lax.fori_loop(0, 2, near_part, p)
        lax.fori_loop(0, 2, far_part, p)
        return carry

    lax.fori_loop(0, 2, pair, 0)

    for g in early:
        early_kv(g).wait_send()
        early_q(g).wait_send()
        for r in range(2):
            out_copy(g, r, None).wait()
    for step in range(3):
        long_q(step).wait_send()
    for g in range(EARLY):
        for r in range(2):
            out_copy(g, r, at(after, z, y)).wait()
        for step in range(3):
            long_out(g, step).wait_send()
        long_out(g, 2).wait_recv()

    def finish(g, carry):
        for src, cond in z_pairs():
            @pl.when(cond)
            def _():
                to_z(g, src).wait_send()
        for src, dst, dy, cond in y_own() + y_near() + y_far():
            @pl.when(cond)
            def _():
                to_y(g, src, dst, dy).wait_send()
        each_pass(g, lambda copy: copy.wait_send())
        return carry

    lax.fori_loop(0, GROUPS, finish, 0)


def local(queries, key_heads, section_values, block_docs):
    bf16, f32 = jnp.bfloat16, jnp.float32
    anywhere = pl.BlockSpec(memory_space=pl.ANY)
    late = GROUPS - EARLY
    dma = pltpu.SemaphoreType.DMA
    out = pl.pallas_call(
        kernel,
        out_shape=jax.ShapeDtypeStruct((TOK, HEADS * D), bf16),
        in_specs=[pl.BlockSpec(memory_space=pltpu.SMEM), anywhere, anywhere, anywhere],
        out_specs=anywhere,
        scratch_shapes=[
            pltpu.VMEM((TOK * HEADS, D), bf16),
            pltpu.VMEM((TOK * GROUPS, D), bf16),
            pltpu.VMEM((TOK * GROUPS, D), bf16),
            pltpu.VMEM((TOK * HEADS, D), f32),
            pltpu.VMEM((HEADS + late * WIDTH, TOK, D), bf16),
            pltpu.VMEM((late, 2, TOK, D), bf16),
            pltpu.VMEM((GROUPS, 9, 2, TOK, D), bf16),
            pltpu.VMEM((NEAR + BLK, 2 * D), bf16),
            pltpu.VMEM((FAR, 2 * D), bf16),
            pltpu.VMEM((TILE, NEAR), f32),
            pltpu.VMEM((TILE, NEAR), f32),
            pltpu.VMEM((TILE, BLK), f32),
            pltpu.VMEM((TILE, BLK), f32),
            pltpu.VMEM((TILE, NEAR), bf16),
            pltpu.VMEM((TILE, NEAR), bf16),
            pltpu.VMEM((2, 2, TILE, 2 * D), f32),
            pltpu.VMEM((2, 2, TILE, D), f32),
            pltpu.VMEM((TILE, 2 * D), f32),
            pltpu.VMEM((GROUPS, TOK, WIDTH * D), bf16),
            pltpu.VMEM((2, LONG, TOK, D), bf16),
            pltpu.VMEM((EARLY, 2, TOK, LONG * D), bf16),
            dma((3,)),
            dma((GROUPS, 9)),
            dma((GROUPS, 9)),
            dma((GROUPS, 2, 2)),
            dma((GROUPS, 2, 2)),
            dma((late,)),
            dma((late,)),
            dma((late,)),
            dma((late,)),
            dma((3,)),
            dma((3,)),
            dma((EARLY, 3)),
            dma((EARLY, 3)),
            dma((EARLY, 2)),
            dma((EARLY, 2)),
            dma((GROUPS, 2)),
        ],
        compiler_params=pltpu.CompilerParams(
            collective_id=0, has_side_effects=True, vmem_limit_bytes=60 * MIB
        ),
    )(
        block_docs,
        queries.reshape(TOK * HEADS, D),
        key_heads.reshape(TOK * GROUPS, D),
        section_values.reshape(TOK * GROUPS, D),
    )
    return out[None]


def solution(mesh):
    specs = P("section", "ctx", "tp", None)
    return jax.shard_map(
        local,
        mesh=mesh,
        in_specs=(specs, specs, specs, P()),
        out_specs=P("section", "ctx", "tp"),
        check_vma=False,
    )
```

time: 62.5 us -> 60.5 us (0.968)
  the two profiles are of different devices: /device:TPU:70 before, /device:TPU:66 now
where the time goes in v3:
time: 60.5 us; the launch traced here: 60.4 us
  Pallas kernels  57.2 us (95%)
  local copies, waits for them, and re-layouts  3.13 us (5%)
    pallas_call x1, Pallas kernels, local(): pl.pallas_call(kernel, out_shape=jax.ShapeDtypeStruct((TOK, HEADS * D), b...  57.2 us
    unnamed x1, local copies, waits for them, and re-layouts  3.13 us

profile of v3, /device:TPU:66, one launch (start us, length us, event | category | flops | bytes accessed | tf_op | source)
XLA Modules:
  0.0 60.4 jit_solution(11718044325741868174)
XLA Ops:
  0.0 57.2 %shard_map.46 = bf16[256,4096]{1,0:T(8,128)(2,1)} custom-call(s32[64]{0:T(128)} %docs.1, bf16[8192,128]{1,0:T(8,128)(2,1)} %bitcast.5, bf16[1024,128]{1,0:T(8,128)(2,1)} %bitcast.6, bf16[1024,128]{1,0:T(8,128)(2,1)} %bitcast.7), custom_call_target="tpu_custom_call" | custom-call | tf_op jit(solution)/shard_map/pallas_call | solution.py:444
  57.2 3.1 %copy.6 = bf16[1,256,4096]{2,1,0:T(8,128)(2,1)} copy(bf16[1,256,4096]{2,1,0:T(8,128)(2,1)} %bitcast.4) | data formatting | bytes 4194304

commit v4 on v3

--- a/solution.py
+++ b/solution.py
@@ -64,7 +64,7 @@
     docs, q_hbm, k_hbm, v_hbm, out_hbm,
     q_in, k_in, v_in, wide, heads, first, kv, va_near, va_far,
     scores_a, scores_b, peaks_a, peaks_b, weights_a, weights_b, kept_mix, kept_peak, far_mix, done, hop_q, hop_o,
-    in_sem, g_send, g_recv, r_send, r_recv, k_send, k_recv, q_send, q_recv, hq_send, hq_recv,
+    in_sem, g_send, g_recv, f_recv, r_send, r_recv, k_send, k_recv, q_send, q_recv, hq_send, hq_recv,
     ho_send, ho_recv, x_send, x_recv, l_sem,
 ):
     sec, ctx, tp = lax.axis_index("section"), lax.axis_index("ctx"), lax.axis_index("tp")
@@ -231,20 +231,53 @@
         long_out(g, step - 1).wait_recv()
         long_out(g, step).start()
 
+    def part_copy(part, src_slot, dst_slot, send_slot, rsem, peer):
+        return remote(kv.at[0, src_slot, part], kv.at[0, dst_slot, part], g_send.at[0, send_slot], rsem, peer)
+
+    def first_z(part):
+        return part_copy(part, 0, 4, 0, f_recv.at[part], at(sec, (z + 1) % NZ, y))
+
+    def first_near(part):
+        @pl.when(z >= 1)
+        def _():
+            first_z(part).wait_recv()
+
+        @pl.when(z_pairs()[1][1])
+        def _():
+            part_copy(part, 4, 8, 1, g_recv.at[0, 8], at(sec, (z + 1) % NZ, y)).start()
+
+        for src, dst, dy, cond in y_near():
+            @pl.when(cond)
+            def _():
+                send_slot = dst + (1 if dst < 4 else 0)
+                peer = at(sec, z, (y + dy) % NY)
+                part_copy(part, src, dst, send_slot, g_recv.at[0, dst], peer).start()
+
     early = range(EARLY, GROUPS)
-    send_z(0, 0)
+
+    @pl.when(z < NZ - 1)
+    def _():
+        for part in range(2):
+            first_z(part).start()
+
     send_own(0)
     send_z(1, 0)
     for g in early:
         early_kv(g).start()
     load_q.wait()
     wide[...] = q_in[...].astype(jnp.float32)
-    for h in [*range(moved, HEADS), *range(moved)]:
+    for h in range(moved, HEADS):
         heads[h] = wide[pl.ds(h, TOK, stride=HEADS), :].astype(jnp.bfloat16)
-        if h >= moved and (h + 1) % WIDTH == 0:
+        if (h + 1) % WIDTH == 0:
             early_q(h // WIDTH).start()
         if h == HEADS - 1:
             long_q(0).start()
+    for part in range(2):
+        first_near(part)
+    send_own(1)
+    send_near(1)
+    for h in range(moved):
+        heads[h] = wide[pl.ds(h, TOK, stride=HEADS), :].astype(jnp.bfloat16)
     va_near[:, D:] = jnp.ones((NEAR + BLK, D), jnp.bfloat16)
     va_far[:, D:] = jnp.ones((FAR, D), jnp.bfloat16)
     for slot in range(1, 8):
@@ -253,9 +286,6 @@
             for g in range(GROUPS):
                 kv[g, slot] = jnp.zeros((2, TOK, D), jnp.bfloat16)
 
-    send_near(0)
-    send_own(1)
-    send_near(1)
     early_kv(2).wait_recv()
     send_z(2, 0)
     early_kv(3).wait_recv()
@@ -323,6 +353,11 @@
             send_near(2)
             send_own(2)
             pass_q(2)
+
+        @pl.when(g == 1)
+        def _():
+            send_near(3)
+            send_own(3)
 
         @pl.when(g == 2)
         def _():
@@ -350,8 +385,6 @@
                 @pl.when(g == 1)
                 def _():
                     send_far(2)
-                    send_near(3)
-                    send_own(3)
 
                 @pl.when(g == 2)
                 def _():
@@ -471,6 +504,7 @@
             dma((3,)),
             dma((GROUPS, 9)),
             dma((GROUPS, 9)),
+            dma((2,)),
             dma((GROUPS, 2, 2)),
             dma((GROUPS, 2, 2)),
             dma((late,)),

time: 60.5 us -> 58.7 us (0.970)
  the two profiles are of different devices: /device:TPU:66 before, /device:TPU:56 now
where the time goes in v4:
time: 58.7 us; the launch traced here: 58.1 us
  Pallas kernels  55 us (94%)
  local copies, waits for them, and re-layouts  3.13 us (5%)
    pallas_call x1, Pallas kernels, local(): pl.pallas_call(kernel, out_shape=jax.ShapeDtypeStruct((TOK, HEADS * D), b...  55 us
    unnamed x1, local copies, waits for them, and re-layouts  3.13 us

profile of v4, /device:TPU:56, one launch (start us, length us, event | category | flops | bytes accessed | tf_op | source)
XLA Modules:
  0.0 58.1 jit_solution(15209537137932139250)
XLA Ops:
  0.0 55.0 %shard_map.46 = bf16[256,4096]{1,0:T(8,128)(2,1)} custom-call(s32[64]{0:T(128)} %docs.1, bf16[8192,128]{1,0:T(8,128)(2,1)} %bitcast.5, bf16[1024,128]{1,0:T(8,128)(2,1)} %bitcast.6, bf16[1024,128]{1,0:T(8,128)(2,1)} %bitcast.7), custom_call_target="tpu_custom_call" | custom-call | tf_op jit(solution)/shard_map/pallas_call | solution.py:477
  55.0 3.1 %copy.6 = bf16[1,256,4096]{2,1,0:T(8,128)(2,1)} copy(bf16[1,256,4096]{2,1,0:T(8,128)(2,1)} %bitcast.4) | data formatting | bytes 4194304
